TPU v7x, 512 devices: a whole 4x4x16 slice. The times are simulated.
512 devices in a mesh: tile: 64 (over z, y_lo, core), led: 8 (over y_hi, x).
Axes of the slice: x: 4, y: 4 (y_hi: 2, y_lo: 2; y = y_hi * 2 + y_lo), z: 16, core: 2. Of those that a mesh axis runs over, the one named last changes fastest.
Arguments:
- spectrum: bfloat16 [64, 2, 512, 512], P('tile'), may hold values from -4 to 4
- pupil: bfloat16 [64, 2, 128, 128], P('tile'), may hold values from -4 to 4
- offsets: int32 [64, 224, 2], P('tile', 'led'), may hold values from 0 to 384, as said below
- widths: int32 [63], replicated, may hold values from 1 to 16
- live: int32 [224], P('led'), may hold values 0 or 1
- measured: bfloat16 [224, 7168, 128], P('led', 'tile'), may hold values from 0 to 2
Outputs:
- spectrum_grad: float32 [64, 2, 512, 512], P('tile', None, 'led')
- pupil_grad: float32 [64, 2, 128, 128], P('tile', None, 'led')
Inputs may be any that keep to these rules, and one draw needn't show every extreme that they name: offsets[t, l] belongs to LED l at row l // 15 and column l % 15 of a 15 x 15 LED grid whose last LED is left out; an LED's offsets vary by at most 16 from tile to tile.
All inputs are finite; a program needn't handle non-finite values. No bound on the sum of `live` on one device may be relied on, other than what follows from the above.
Results may differ from a plain program's by a relative error of at most 0.0003.
Values may be sent and summed in bfloat16 or wider, within the bound.
A program may use at most 64 MiB of HBM per device.

v0:
```python
from functools import partial
import math

import jax
import jax.numpy as jnp
from jax import lax
from jax.sharding import PartitionSpec as P

PUP = 128
OV = 16


def with_halo(x, sides, width):
    for axis, dim in sides:
        size, length = (lax.axis_size(axis), x.shape[dim])
        up = [(i, (i + 1) % size) for i in range(size - 1)]
        down = [(j, i) for i, j in up]
        last = lax.slice_in_dim(x, length - width, length, axis=dim)
        initial = lax.slice_in_dim(x, 0, width, axis=dim)
        before = lax.ppermute(last, axis, up)
        after = lax.ppermute(initial, axis, down)
        x = jnp.concatenate([before, x, after], axis=dim)
    return x


def blend_weights(widths, index, tiles):
    rows = jnp.arange(PUP)
    place = rows.astype(jnp.float32)
    half = OV // 2
    stride = PUP - OV
    above_width = widths[jnp.maximum(index - 1, 0)].astype(jnp.float32)
    below_width = widths[jnp.minimum(index, tiles - 2)].astype(jnp.float32)
    ramp_above = jnp.clip(0.5 + (half - 0.5 - place) / above_width, 0.0, 1.0)
    ramp_below = jnp.clip(0.5 + (half - 0.5 - (place - stride)) / below_width, 0.0, 1.0)
    weights = jnp.where((rows < OV) & (index > 0), 1.0 - ramp_above, jnp.ones_like(ramp_above))
    weights = jnp.where((rows >= stride) & (index < tiles - 1), ramp_below, weights)
    return weights


def dft_tables(length):
    products = jnp.arange(length)[:, None] * jnp.arange(length)[None, :] % length
    angle = products.astype(jnp.float32) * (2.0 * math.pi / length)
    cosine = jnp.cos(angle) / math.sqrt(length)
    sine = jnp.sin(angle) / math.sqrt(length)
    left = jnp.stack([jnp.stack([cosine, -sine]), jnp.stack([sine, cosine])])
    right = jnp.stack([jnp.stack([cosine, sine]), jnp.stack([-sine, cosine])])
    return (left, right)


def take_window(source, start):
    zero = jnp.zeros((), jnp.int32)
    return lax.dynamic_slice(source, (zero, start[0], start[1]), (2, PUP, PUP))


def add_window(total, piece, start):
    zero = jnp.zeros((), jnp.int32)
    place = (zero, start[0], start[1])
    current = lax.dynamic_slice(total, place, piece.shape)
    return lax.dynamic_update_slice(total, current + piece, place)


def on_device(spectrum, pupil, offsets, widths, live, measured):
    tiles = lax.axis_size("tile")
    index = lax.axis_index("tile")
    groups = lax.axis_size("led")
    spec_data = spectrum[0].astype(jnp.float32)
    pupil_data = pupil[0].astype(jnp.float32)
    side = spec_data.shape[-1]
    length = pupil_data.shape[-1]
    half = OV // 2
    stride = length - OV
    lamps = measured.shape[0]
    scale = 1.0 / math.sqrt(lamps * groups)
    highest = lax.Precision.HIGHEST
    starts = offsets[0]
    windows = jax.vmap(partial(take_window, spec_data))(starts)
    pupil_re = pupil_data[0]
    pupil_im = pupil_data[1]
    crop_re = windows[:, 0]
    crop_im = windows[:, 1]
    field = jnp.stack(
        [pupil_re * crop_re - pupil_im * crop_im, pupil_re * crop_im + pupil_im * crop_re], 1
    )
    left, right = dft_tables(length)
    mixed = jnp.einsum("qpab,lpbc->lqac", left, field, precision=highest)
    wave = jnp.einsum("lpac,pqcd->lqad", mixed, right, precision=highest)
    intensity = wave[:, 0] * wave[:, 0] + wave[:, 1] * wave[:, 1]
    weights = blend_weights(widths, index, tiles)[None, :, None]
    weighted = weights * intensity
    alive = (scale * live.astype(jnp.float32))[:, None, None]
    extended = with_halo(weighted.astype(jnp.bfloat16), (("tile", 1),), half).astype(weighted.dtype)
    above = jnp.pad(extended[:, :half], ((0, 0), (0, stride - half), (0, 0)))
    below = jnp.pad(extended[:, length + half :], ((0, 0), (stride - half, 0), (0, 0)))
    blended = weighted[:, half : half + stride] + above + below
    residual = alive * (blended - measured.astype(jnp.float32))
    local = with_halo(residual, (("tile", 1),), half)
    grad_int = weights * local
    grad_wave = (2.0 * grad_int)[:, None] * wave
    back = jnp.einsum("lqad,pqcd->lpac", grad_wave, right, precision=highest)
    grad_field = jnp.einsum("qpab,lqac->lpbc", left, back, precision=highest)
    grad_re = grad_field[:, 0]
    grad_im = grad_field[:, 1]
    crop_grad = jnp.stack(
        [pupil_re * grad_re + pupil_im * grad_im, pupil_re * grad_im - pupil_im * grad_re], 1
    )
    pupil_part = jnp.stack(
        [
            jnp.sum(crop_re * grad_re + crop_im * grad_im, 0),
            jnp.sum(crop_re * grad_im - crop_im * grad_re, 0),
        ],
        0,
    )

    def place_one(number, total):
        return add_window(total, crop_grad[number], starts[number])

    spec_part = lax.fori_loop(0, lamps, place_one, jnp.zeros((2, side, side), jnp.float32))
    spec_share, pupil_share = (
        lax.psum_scatter(spec_part, "led", scatter_dimension=1, tiled=True),
        lax.psum_scatter(pupil_part, "led", scatter_dimension=1, tiled=True),
    )
    return (spec_share[None], pupil_share[None])


def solution(mesh):
    return jax.shard_map(
        on_device,
        mesh=mesh,
        in_specs=(
            P("tile", None, None, None),
            P("tile", None, None, None),
            P("tile", "led", None),
            P(),
            P("led"),
            P("led", "tile", None),
        ),
        out_specs=(P("tile", None, "led", None), P("tile", None, "led", None)),
        check_vma=False,
    )
```

profile of v0, /device:TPU:1, one launch (start us, length us, event | category | flops | bytes accessed | tf_op | source)
XLA Modules:
  0.0 464.8 jit_solution(14302707311443478207)
XLA Ops:
  10.1 78.3 %while.15 = (s32[]{:T(128)}, f32[2,512,512]{2,1,0:T(8,128)S(1)}, s32[28,3]{0,1:T(4,128)S(1)}, f32[28,2,128,128]{2,3,1,0:T(8,128)}, s32[]{:T(128)}) while((s32[]{:T(128)}, f32[2,512,512]{2,1,0:T(8,128)S(1)}, s32[28,3]{0,1:T(4,128)S(1)}, f32[28,2,128,128]{2,3,1,0:T(8,128)}, s32[]{:T(128)}) %tuple.70), condition=%wide.while_cond, body=%wide.while_body.sunk | while | flops 2 | bytes 787057 | solution.py:52
  90.5 2.7 multiply_subtract_fusion.1
  93.2 3.3 fusion
  96.5 6.1 %fusion.9 = f32[28,2,128,128]{3,2,0,1:T(8,128)S(1)} fusion(f32[28,128,2,128,1]{3,1,4,2,0:T(8,128)S(1)} %fusion, f32[1,2,128,128]{3,2,1,0:T(8,128)S(1)} %get-tuple-element.147, f32[1,2,128,128]{3,2,1,0:T(8,128)S(1)} %get-tuple-element.140), kind=kOutput, calls=%fused_computation.18 | convolution fusion | flops 2818637824 | bytes 7602176 | tf_op jit(solution)/shard_map/lpac,pqcd->lqad/dot_general | solution.py:86
  104.5 4.6 collective-permute-start
  109.1 5.7 %collective-permute-start.1 = (bf16[28,8,128]{2,1,0:T(8,128)(2,1)S(1)}, bf16[28,8,128]{2,1,0:T(8,128)(2,1)S(1)}, u32[]{:S(2)}, u32[]{:S(2)}) collective-permute-start(bf16[28,8,128]{2,1,0:T(8,128)(2,1)S(1)} %get-tuple-element.139), channel_id=1, source_target_pairs={{8,0},{16,8},{24,16},{32,24},{40,32},{48,40},{56,48},{64,56},{72,6... | collective-permute-start | bytes 172040 | tf_op jit(solution)/shard_map/ppermute | solution.py:21
  121.4 3.9 collective-permute-done.3
  125.6 3.4 fusion.7
  129.1 3.2 fusion.12
  135.3 3.6 pad_maximum_fusion
  139.6 223.6 %while.14 = (s32[]{:T(128)}, f32[2,512,512]{2,1,0:T(8,128)S(1)}, s32[28,2]{0,1:T(2,128)S(1)}, f32[28,2,128,128]{2,3,1,0:T(8,128)}, s32[]{:T(128)}, /*index=5*/s32[]{:T(128)}, s32[]{:T(128)}) while((s32[]{:T(128)}, f32[2,512,512]{2,1,0:T(8,128)S(1)}, s32[28,2]{0,1:T(2,128)S(1)}, f32[28,2,128,128]{2,3,1,0:T(8,128)}, s32[]{:T(128)}, ...), condition=%wide.region_1.2_spmd, body=%wide.region_0.1_spmd.sunk | while | flops 32776 | bytes 1179845 | solution.py:117
  152.5 2.5 dynamic_update_slice.8
  160.6 2.5 dynamic_update_slice.8
  168.8 2.5 dynamic_update_slice.8
  176.9 2.5 dynamic_update_slice.8
  185.0 2.5 dynamic_update_slice.8
  193.1 2.5 dynamic_update_slice.8
  201.2 2.5 dynamic_update_slice.8
  209.3 2.5 dynamic_update_slice.8
  217.4 2.5 dynamic_update_slice.8
  225.6 2.5 dynamic_update_slice.8
  280.3 2.5 dynamic_update_slice.8
  288.4 2.5 dynamic_update_slice.8
  296.5 2.5 dynamic_update_slice.8
  312.0 2.5 dynamic_update_slice.8
  320.1 2.5 dynamic_update_slice.8
  328.2 2.5 dynamic_update_slice.8
  336.4 2.5 dynamic_update_slice.8
  344.5 2.5 dynamic_update_slice.8
  352.6 2.5 dynamic_update_slice.8
  360.7 2.5 dynamic_update_slice.8
  367.9 90.1 %reduce-scatter.2.cloned.1.call-done = f32[2,64,512]{2,1,0:T(8,128)} async-done(((f32[2,512,512]{2,1,0:T(8,128)}), f32[2,64,512]{2,1,0:T(8,128)}) %reduce-scatter.2.cloned.1.call-update) | async-done | bytes 262160 | tf_op jit(solution)/shard_map/reduce_scatter | solution.py:119
  (347 shorter events, 163.8 us)
Async XLA Ops:
  7.2 359.4 %all-reduce.4.cloned.1.call-start = ((), (), s32[]{:S(2)}) async-start(), calls=%async_computation.2 | async-start | bytes 262144
  10.1 78.3 %copy-start.5 = (bf16[1,2,128,128]{3,2,1,0:T(8,128)(2,1)S(1)}, bf16[1,2,128,128]{3,2,1,0:T(8,128)(2,1)}, u32[]{:S(2)}) copy-start(bf16[1,2,128,128]{3,2,1,0:T(8,128)(2,1)} %param.9) | copy-start | bytes 196612
  10.1 78.5 %copy-start.7 = (s32[63]{0:T(128)S(1)}, s32[63]{0:T(128)}, u32[]{:S(2)}) copy-start(s32[63]{0:T(128)} %param.11) | copy-start | bytes 760
  102.7 1.8 copy-start
  102.7 12.1 %copy-start.9 = (s32[28]{0:T(128)S(1)}, s32[28]{0:T(128)}, u32[]{:S(2)}) copy-start(s32[28]{0:T(128)} %param.12) | copy-start | bytes 340
  104.5 10.3 %collective-permute-start = (bf16[28,8,128]{2,1,0:T(8,128)(2,1)S(1)}, bf16[28,8,128]{2,1,0:T(8,128)(2,1)S(1)}, u32[]{:S(2)}, u32[]{:S(2)}) collective-permute-start(bf16[28,8,128]{2,1,0:T(8,128)(2,1)S(1)} %get-tuple-element.138), channel_id=1, source_target_pairs={{0,8},{8,16},{16,24},{24,32},{32,40},{40,48},{48,56},{56,64},{64,7... | collective-permute-start | bytes 172040 | tf_op jit(solution)/shard_map/ppermute | solution.py:20
  109.1 6.4 %collective-permute-start.1 = (bf16[28,8,128]{2,1,0:T(8,128)(2,1)S(1)}, bf16[28,8,128]{2,1,0:T(8,128)(2,1)S(1)}, u32[]{:S(2)}, u32[]{:S(2)}) collective-permute-start(bf16[28,8,128]{2,1,0:T(8,128)(2,1)S(1)} %get-tuple-element.139), channel_id=1, source_target_pairs={{8,0},{16,8},{24,16},{32,24},{40,32},{48,40},{56,48},{64,56},{72,6... | collective-permute-start | bytes 172040 | tf_op jit(solution)/shard_map/ppermute | solution.py:21
  115.5 1.1 copy-start.4
  115.5 1.1 copy-start.8
  117.1 4.4 collective-permute-start.2
  119.0 6.3 %collective-permute-start.3 = (f32[28,8,128]{2,1,0:T(8,128)S(1)}, f32[28,8,128]{2,1,0:T(8,128)S(1)}, u32[]{:S(2)}, u32[]{:S(2)}) collective-permute-start(f32[28,8,128]{2,1,0:T(8,128)S(1)} %get-tuple-element.137), channel_id=1, source_target_pairs={{8,0},{16,8},{24,16},{32,24},{40,32},{48,40},{56,48},{64,56},{72,6... | collective-permute-start | bytes 344072 | tf_op jit(solution)/shard_map/ppermute | solution.py:21
  121.4 4.2 copy-start.1
  129.1 3.2 copy-start.2
  135.2 322.8 %reduce-scatter.2.cloned.1.call-start = ((), (), s32[]{:S(2)}) async-start(), calls=%async_computation.1 | async-start | bytes 2359296 | tf_op jit(solution)/shard_map/reduce_scatter | solution.py:119
  138.9 0.7 copy-start.6
  363.2 1.3 copy-start.3
Sparse Core Ops, SparseCore 0:
  135.4 99.9 all-reduce.3
  364.7 93.2 reduce-scatter.1
where the time goes:
time: 468 us; the launch traced here: 465 us
  local copies, waits for them, and re-layouts  199 us (43%)
  loops' own time  108 us (23%)
  waiting for transfers between devices  94.7 us (20%)
  between operations  16.4 us (4%)
  matrix products  16 us (3%)
  other arithmetic  15.9 us (3%)
  starting transfers between devices  14.7 us (3%)
    another operation x1, loops' own time, on_device(): lax.fori_loop(0, lamps, place_one, jnp.zeros((2, side, side), jnp.float32))  108 us
    reduce_scatter x1, waiting for transfers between devices, on_device(): lax.psum_scatter(spec_part, 'led', scatter_dimension=1, tiled=True)  90.1 us
    gather x140, local copies, waits for them, and re-layouts  77.8 us
    dynamic_update_slice x28, local copies, waits for them, and re-layouts, add_window(): return lax.dynamic_update_slice(total, current + piece, place)  66.2 us
    dynamic_slice x84, local copies, waits for them, and re-layouts, place_one(): return add_window(total, crop_grad[number], starts[number])  30.5 us
    slice x28, local copies, waits for them, and re-layouts, add_window(): place = (zero, start[0], start[1])  16 us
  transfers between devices with their start and end apart: 6, of which 3 were waited for; matrix products, arithmetic and copies ran while one was open for 26% of the time, Pallas kernels for 0%

commit v1 on v0

v1 whole, which is shorter than its diff:
```python
from functools import partial
import math

import jax
import jax.numpy as jnp
import ml_dtypes
import numpy as np
from jax import lax
from jax.experimental import pallas as pl
from jax.experimental.pallas import tpu as pltpu
from jax.sharding import PartitionSpec as P

PUP = 128
OV = 16
HALF = 8
STRIDE = PUP - OV
BLOCKS = 4
MESH = pl.DeviceIdType.MESH
F32 = jnp.float32
BF16 = jnp.bfloat16
PAIRS = 2
GROUP = 2 * PAIRS
VMEM_LIMIT = 48 * 1024 * 1024


def dft_tables():
    k = np.arange(PUP)
    angle = 2.0 * np.pi * ((k[:, None] * k[None, :]) % PUP) / PUP
    cosine, sine = np.cos(angle), np.sin(angle)
    inverse = np.block([[cosine, sine], [-sine, cosine]]) / PUP
    forward = np.block([[cosine, -sine], [sine, cosine]])
    parts = []
    for table in (inverse, forward):
        high = table.astype(ml_dtypes.bfloat16)
        low = (table - high.astype(np.float64)).astype(ml_dtypes.bfloat16)
        parts += [high, low]
    return np.stack(parts)


def split(x):
    high = x.astype(BF16)
    return high, (x - high.astype(F32)).astype(BF16)


def right_product(x, high, low):
    xh, xl = split(x)
    data = jnp.concatenate([xh, xl, xh], axis=1)
    table = jnp.concatenate([high, high, low], axis=0)
    return jnp.dot(data, table, preferred_element_type=F32)


def left_product(high, low, x):
    xh, xl = split(x)
    data = jnp.concatenate([xh, xl, xh], axis=0)
    table = jnp.concatenate([high, high, low], axis=1)
    return jnp.dot(table, data, preferred_element_type=F32)


def swap_blocks(x):
    top = jnp.concatenate([x[:PUP, :PUP], x[PUP:, :PUP]], axis=1)
    bottom = jnp.concatenate([x[:PUP, PUP:], x[PUP:, PUP:]], axis=1)
    return jnp.concatenate([top, bottom], axis=0)


def ramp_weights(widths_ref, tile, tiles):
    place = lax.broadcasted_iota(jnp.int32, (OV, PUP), 0).astype(F32)
    above = widths_ref[jnp.maximum(tile - 1, 0)].astype(F32)
    below = widths_ref[jnp.minimum(tile, tiles - 2)].astype(F32)
    top = 1.0 - jnp.clip(0.5 + (HALF - 0.5 - place) / above, 0.0, 1.0)
    bottom = jnp.clip(0.5 + (HALF - 0.5 - place) / below, 0.0, 1.0)
    ones = jnp.ones_like(place)
    return jnp.where(tile > 0, top, ones), jnp.where(tile < tiles - 1, bottom, ones)


def list_live(live_ref, order_ref):
    def body(led, count):
        order_ref[count] = led
        return count + live_ref[led]

    lamps = live_ref.shape[0]
    count = lax.fori_loop(0, lamps, body, jnp.int32(0))
    for extra in range(GROUP):
        order_ref[count + extra] = 0
    return count


def load_spectrum(spec_ref, planes):
    for block in range(BLOCKS):
        for part in range(2):
            planes[block, part] = spec_ref[part, :, block * PUP : (block + 1) * PUP].astype(F32)


def window_of(planes, row, col):
    first = col // PUP
    second = jnp.minimum(first + 1, BLOCKS - 1)
    lanes = lax.broadcasted_iota(jnp.int32, (PUP, PUP), 1)
    inside = lanes >= col % PUP
    return [
        jnp.where(inside, planes[first, part, pl.ds(row, PUP), :], planes[second, part, pl.ds(row, PUP), :])
        for part in range(2)
    ]


def forward_kernel(offsets_ref, widths_ref, live_ref, spec_ref, pupil_ref, table_ref, wave_out, edge_out, planes, waves, order_ref, sems):
    tiles = lax.axis_size("tile")
    tile = lax.axis_index("tile")
    count = list_live(live_ref, order_ref)
    load_spectrum(spec_ref, planes)
    top, bottom = ramp_weights(widths_ref, tile, tiles)
    top2 = jnp.concatenate([top, top], axis=1)
    bottom2 = jnp.concatenate([bottom, bottom], axis=1)

    def field_of(slot):
        led = order_ref[slot]
        row, col = offsets_ref[led, 0], offsets_ref[led, 1]
        win_re, win_im = window_of(planes, row, col)
        shift = col % PUP
        pup_re = pltpu.roll(pupil_ref[0].astype(F32), shift, axis=1)
        pup_im = pltpu.roll(pupil_ref[1].astype(F32), shift, axis=1)
        return jnp.concatenate(
            [pup_re * win_re - pup_im * win_im, pup_re * win_im + pup_im * win_re], axis=1
        )

    def step(number, carry):
        for inner in range(PAIRS):
            pair = number * PAIRS + inner
            field = jnp.concatenate([field_of(2 * pair), field_of(2 * pair + 1)], axis=0)
            mixed = right_product(field, table_ref[0], table_ref[1])
            wave = left_product(table_ref[2], table_ref[3], swap_blocks(mixed))
            waves[pair] = wave
            first = wave[:OV], wave[PUP : PUP + OV]
            last = wave[STRIDE:PUP], wave[PUP + STRIDE :]
            edge_out[0, pair] = top2 * (first[0] * first[0] + first[1] * first[1])
            edge_out[1, pair] = bottom2 * (last[0] * last[0] + last[1] * last[1])
        here = pl.ds(number * PAIRS, PAIRS)
        pltpu.make_async_copy(waves.at[here], wave_out.at[here], sems.at[number]).start()
        return carry

    steps = (count + GROUP - 1) // GROUP
    lax.fori_loop(0, steps, step, 0)

    def finish(number, carry):
        here = pl.ds(number * PAIRS, PAIRS)
        pltpu.make_async_copy(waves.at[here], wave_out.at[here], sems.at[number]).wait()
        return carry

    lax.fori_loop(0, steps, finish, 0)


def backward_kernel(
    scale, offsets_ref, widths_ref, live_ref, spec_ref, pupil_ref, table_ref, measured_ref, above_ref, below_ref, edge_ref, wave_in,
    spec_out, pupil_out, planes, waves, order_ref, sems
):
    tiles = lax.axis_size("tile")
    tile = lax.axis_index("tile")
    count = list_live(live_ref, order_ref)
    steps = (count + GROUP - 1) // GROUP

    def fetch(number, carry):
        here = pl.ds(number * PAIRS, PAIRS)
        pltpu.make_async_copy(wave_in.at[here], waves.at[here], sems.at[number]).start()
        return carry

    lax.fori_loop(0, steps, fetch, 0)
    load_spectrum(spec_ref, planes)
    spec_out[...] = jnp.zeros_like(spec_out)
    pupil_out[...] = jnp.zeros_like(pupil_out)
    top, bottom = ramp_weights(widths_ref, tile, tiles)
    top2 = jnp.concatenate([top, top], axis=1)
    bottom2 = jnp.concatenate([bottom, bottom], axis=1)
    rows = lax.broadcasted_iota(jnp.int32, (OV, 2 * PUP), 0)
    top_grad = jnp.where((tile > 0) | (rows >= HALF), 2.0 * top2, 0.0)
    bottom_grad = jnp.where((tile < tiles - 1) | (rows < HALF), 2.0 * bottom2, 0.0)
    has_above = tile > 0
    has_below = tile < tiles - 1
    lanes = lax.broadcasted_iota(jnp.int32, (PUP, PUP), 1)

    def images(ref, leds, low, high):
        return jnp.concatenate([ref[led, low:high].astype(F32) for led in leds], axis=1)

    def step(number, carry):
        here = pl.ds(number * PAIRS, PAIRS)
        pltpu.make_async_copy(wave_in.at[here], waves.at[here], sems.at[number]).wait()
        for inner in range(PAIRS):
            pair = number * PAIRS + inner
            leds = order_ref[2 * pair], order_ref[2 * pair + 1]
            side_of = lax.broadcasted_iota(jnp.int32, (1, 2 * PUP), 1) // PUP
            alive = jnp.where(2 * pair + side_of < count, scale, 0.0)
            wave = waves[pair]
            wave_re, wave_im = wave[:PUP], wave[PUP:]
            intensity = wave_re * wave_re + wave_im * wave_im
            own = images(measured_ref, leds, 0, STRIDE)
            upper = images(above_ref, leds, OV - HALF, OV)
            lower = images(below_ref, leds, 0, HALF)
            near_top = jnp.where(has_above, edge_ref[1, pair], 0.0)
            near_bottom = jnp.where(has_below, edge_ref[0, pair], 0.0)
            first = top_grad * (top2 * intensity[:OV] + near_top - jnp.concatenate([upper, own[: OV - HALF]], axis=0))
            middle = 2.0 * (intensity[OV:STRIDE] - own[HALF : STRIDE - HALF])
            last = bottom_grad * (bottom2 * intensity[STRIDE:] + near_bottom - jnp.concatenate([own[STRIDE - HALF :], lower], axis=0))
            grad = alive * jnp.concatenate([first, middle, last], axis=0)
            grad_wave = jnp.concatenate([grad * wave_re, grad * wave_im], axis=0)
            back = right_product(swap_blocks(grad_wave), table_ref[2], table_ref[3])
            grad_field = left_product(table_ref[0], table_ref[1], swap_blocks(back))
            for side in range(2):
                led = leds[side]
                row, col = offsets_ref[led, 0], offsets_ref[led, 1]
                shift = col % PUP
                lo = side * PUP
                grad_re = grad_field[:PUP, lo : lo + PUP]
                grad_im = grad_field[PUP:, lo : lo + PUP]
                pup_re = pltpu.roll(pupil_ref[0].astype(F32), shift, axis=1)
                pup_im = pltpu.roll(pupil_ref[1].astype(F32), shift, axis=1)
                win_re, win_im = window_of(planes, row, col)
                pieces = (pup_re * grad_re + pup_im * grad_im, pup_re * grad_im - pup_im * grad_re)
                shares = (win_re * grad_re + win_im * grad_im, win_re * grad_im - win_im * grad_re)
                first_block = col // PUP
                second_block = jnp.minimum(first_block + 1, BLOCKS - 1)
                inside = lanes >= shift
                for part in range(2):
                    here_rows = pl.ds(row, PUP)
                    pupil_out[part] += pltpu.roll(shares[part], PUP - shift, axis=1)
                    spec_out[first_block, part, here_rows, :] += jnp.where(inside, pieces[part], 0.0)
                    spec_out[second_block, part, here_rows, :] += jnp.where(inside, 0.0, pieces[part])
        return carry

    lax.fori_loop(0, steps, step, 0)


def vmem():
    return pl.BlockSpec(memory_space=pltpu.VMEM)


def smem():
    return pl.BlockSpec(memory_space=pltpu.SMEM)


def hbm():
    return pl.BlockSpec(memory_space=pl.ANY)


def forward_call(offsets, widths, live, spectrum, pupil, tables):
    lamps = offsets.shape[0]
    side = spectrum.shape[-1]
    chunks = -(-lamps // GROUP)
    pairs = chunks * PAIRS
    return pl.pallas_call(
        forward_kernel,
        out_shape=(
            jax.ShapeDtypeStruct((pairs, 2 * PUP, 2 * PUP), F32),
            jax.ShapeDtypeStruct((2, pairs, OV, 2 * PUP), F32),
        ),
        in_specs=[smem()] * 3 + [vmem()] * 3,
        out_specs=(hbm(), vmem()),
        scratch_shapes=[
            pltpu.VMEM((BLOCKS, 2, side, PUP), F32),
            pltpu.VMEM((pairs, 2 * PUP, 2 * PUP), F32),
            pltpu.SMEM((lamps + GROUP,), jnp.int32),
            pltpu.SemaphoreType.DMA((chunks,)),
        ],
        compiler_params=pltpu.CompilerParams(vmem_limit_bytes=VMEM_LIMIT),
        name="forward",
    )(offsets, widths, live, spectrum, pupil, tables)


def backward_call(scale, offsets, widths, live, spectrum, pupil, tables, measured, above, below, edges, waves):
    lamps = offsets.shape[0]
    side = spectrum.shape[-1]
    chunks = -(-lamps // GROUP)
    pairs = chunks * PAIRS
    return pl.pallas_call(
        partial(backward_kernel, scale),
        out_shape=(
            jax.ShapeDtypeStruct((BLOCKS, 2, side, PUP), F32),
            jax.ShapeDtypeStruct((2, PUP, PUP), F32),
        ),
        in_specs=[smem()] * 3 + [vmem()] * 7 + [hbm()],
        out_specs=(vmem(), vmem()),
        scratch_shapes=[
            pltpu.VMEM((BLOCKS, 2, side, PUP), F32),
            pltpu.VMEM((pairs, 2 * PUP, 2 * PUP), F32),
            pltpu.SMEM((lamps + GROUP,), jnp.int32),
            pltpu.SemaphoreType.DMA((chunks,)),
        ],
        compiler_params=pltpu.CompilerParams(vmem_limit_bytes=VMEM_LIMIT),
        name="backward",
    )(offsets, widths, live, spectrum, pupil, tables, measured, above, below, edges, waves)


def exchange_kernel(edge_ref, measured_ref, near_ref, above_ref, below_ref, send_sems, recv_sems):
    tiles = lax.axis_size("tile")
    me = lax.axis_index("tile")
    up, down = lax.rem(me + tiles - 1, tiles), lax.rem(me + 1, tiles)
    barrier = pltpu.get_barrier_semaphore()
    for other in (up, down):
        pl.semaphore_signal(barrier, inc=1, device_id={"tile": other}, device_id_type=MESH)
    pl.semaphore_wait(barrier, 2)

    def send(number, source, target, other):
        return pltpu.make_async_remote_copy(
            src_ref=source, dst_ref=target, send_sem=send_sems.at[number], recv_sem=recv_sems.at[number],
            device_id={"tile": other}, device_id_type=MESH,
        )

    copies = [
        send(0, edge_ref.at[0], near_ref.at[0], up),
        send(1, edge_ref.at[1], near_ref.at[1], down),
        send(2, measured_ref.at[:, pl.ds(0, OV)], below_ref, up),
        send(3, measured_ref.at[:, pl.ds(STRIDE - OV, OV)], above_ref, down),
    ]
    for copy in copies:
        copy.start()
    for copy in copies:
        copy.wait()


def exchange_call(edges, measured):
    lamps = measured.shape[0]
    rows = jax.ShapeDtypeStruct((lamps, OV, PUP), measured.dtype)
    return pl.pallas_call(
        exchange_kernel,
        out_shape=(jax.ShapeDtypeStruct(edges.shape, edges.dtype), rows, rows),
        in_specs=[hbm()] * 2,
        out_specs=(hbm(), hbm(), hbm()),
        scratch_shapes=[pltpu.SemaphoreType.DMA((4,)), pltpu.SemaphoreType.DMA((4,))],
        compiler_params=pltpu.CompilerParams(collective_id=1, has_side_effects=True),
        name="exchange",
    )(edges, measured)


LEVELS = 32767.0


def gather_kernel(groups, spec_ref, pupil_ref, spec_out, pupil_out, codes, scales, held, held_scales, held_pupil, send_sems, recv_sems):
    me = lax.axis_index("led")
    depth = spec_ref.shape[2] // groups
    width = pupil_ref.shape[1] // groups

    def peer(step):
        return lax.rem(me + step, groups)

    barrier = pltpu.get_barrier_semaphore()
    for step in range(1, groups):
        pl.semaphore_signal(barrier, inc=1, device_id={"led": peer(step)}, device_id_type=MESH)
    pl.semaphore_wait(barrier, groups - 1)

    def copies(step):
        other = peer(step)
        slot = groups - step
        sources = (codes.at[step - 1], scales.at[step - 1], pupil_ref.at[:, pl.ds(pl.multiple_of(other * width, width), width)])
        targets = (held.at[step - 1], held_scales.at[step - 1], held_pupil.at[step - 1])
        return [
            pltpu.make_async_remote_copy(
                src_ref=source, dst_ref=target, send_sem=send_sems.at[step - 1, kind], recv_sem=recv_sems.at[step - 1, kind],
                device_id={"led": other}, device_id_type=MESH,
            )
            for kind, (source, target) in enumerate(zip(sources, targets))
        ]

    for step in range(1, groups):
        start = pl.multiple_of(peer(step) * depth, depth)
        for block in range(BLOCKS):
            for part in range(2):
                x = spec_ref[block, part, pl.ds(start, depth), :]
                most = jnp.maximum(jnp.max(jnp.abs(x), axis=0, keepdims=True), 1e-30)
                codes[step - 1, block, part] = jnp.round(x * (LEVELS / most)).astype(jnp.int16)
                scales[step - 1, block * 2 + part : block * 2 + part + 1, :] = most * (1.0 / LEVELS)
        for copy in copies(step):
            copy.start()
    mine = pl.multiple_of(me * depth, depth)
    for part in range(2):
        pupil_out[part] = pupil_ref[part, pl.ds(pl.multiple_of(me * width, width), width)]
        for block in range(BLOCKS):
            spec_out[part, :, block * PUP : (block + 1) * PUP] = spec_ref[block, part, pl.ds(mine, depth), :]
    for step in range(1, groups):
        for copy in copies(step):
            copy.wait()
        for part in range(2):
            pupil_out[part] += held_pupil[step - 1, part]
            for block in range(BLOCKS):
                scale = held_scales[step - 1, block * 2 + part : block * 2 + part + 1, :]
                spec_out[part, :, block * PUP : (block + 1) * PUP] += held[step - 1, block, part].astype(F32) * scale


def gather_call(spec_part, pupil_part, groups):
    blocks, parts, side, _ = spec_part.shape
    depth, width = side // groups, PUP // groups
    others = groups - 1
    return pl.pallas_call(
        partial(gather_kernel, groups),
        out_shape=(
            jax.ShapeDtypeStruct((parts, depth, blocks * PUP), F32),
            jax.ShapeDtypeStruct((parts, width, PUP), F32),
        ),
        in_specs=[vmem(), vmem()],
        out_specs=(vmem(), vmem()),
        scratch_shapes=[
            pltpu.VMEM((others, blocks, parts, depth, PUP), jnp.int16),
            pltpu.VMEM((others, blocks * parts, PUP), F32),
            pltpu.VMEM((others, blocks, parts, depth, PUP), jnp.int16),
            pltpu.VMEM((others, blocks * parts, PUP), F32),
            pltpu.VMEM((others, parts, width, PUP), F32),
            pltpu.SemaphoreType.DMA((others, 3)),
            pltpu.SemaphoreType.DMA((others, 3)),
        ],
        compiler_params=pltpu.CompilerParams(
            collective_id=2, has_side_effects=True, vmem_limit_bytes=VMEM_LIMIT
        ),
        name="reduce_scatter",
    )(spec_part, pupil_part)


def on_device(tables, spectrum, pupil, offsets, widths, live, measured):
    groups = lax.axis_size("led")
    lamps = measured.shape[0]
    scale = 1.0 / math.sqrt(lamps * groups)
    spectrum, pupil, offsets = spectrum[0], pupil[0], offsets[0]
    waves, edges = forward_call(offsets, widths, live, spectrum, pupil, tables)
    near, above, below = exchange_call(edges, measured)
    spec_part, pupil_part = backward_call(
        scale, offsets, widths, live, spectrum, pupil, tables, measured, above, below, near, waves
    )
    spec_share, pupil_share = gather_call(spec_part, pupil_part, groups)
    return spec_share[None], pupil_share[None]


def solution(mesh):
    tables = dft_tables()

    def run(spectrum, pupil, offsets, widths, live, measured):
        return jax.shard_map(
            on_device,
            mesh=mesh,
            in_specs=(
                P(),
                P("tile", None, None, None),
                P("tile", None, None, None),
                P("tile", "led", None),
                P(),
                P("led"),
                P("led", "tile", None),
            ),
            out_specs=(P("tile", None, "led", None), P("tile", None, "led", None)),
            check_vma=False,
        )(jnp.asarray(tables), spectrum, pupil, offsets, widths, live, measured)

    return run
```

time: 468 us -> 70.3 us (0.15)
  the two profiles are of different devices: /device:TPU:1 before, /device:TPU:257 now
where the time goes in v1:
time: 70.3 us; the launch traced here: 69.7 us
  Pallas kernels  51.6 us (73%)
  local copies, waits for them, and re-layouts  17.4 us (25%)
    pallas_call x1, Pallas kernels, gather_call(): pl.pallas_call(partial(gather_kernel, groups), out_shape=(jax.ShapeDtypeS...  28.3 us
    unnamed x34, local copies, waits for them, and re-layouts  16.6 us
    pallas_call x1, Pallas kernels, exchange_call(): pl.pallas_call(exchange_kernel, out_shape=(jax.ShapeDtypeStruct(edges.sha...  11.6 us
    pallas_call x1, Pallas kernels, backward_call(): pl.pallas_call(partial(backward_kernel, scale), out_shape=(jax.ShapeDtype...  6.53 us
    pallas_call x1, Pallas kernels, forward_call(): pl.pallas_call(forward_kernel, out_shape=(jax.ShapeDtypeStruct((pairs, 2...  5.22 us

profile of v1, /device:TPU:257, one launch (start us, length us, event | category | flops | bytes accessed | tf_op | source)
XLA Modules:
  0.0 69.7 jit_solution(793407519485911753)
XLA Ops:
  0.6 0.8 %copy.10.offsets_ref = s32[28,2]{1,0:T(8,128)S(1)} copy(s32[28,2]{0,1:T(2,128)} %bitcast.11) | data formatting | bytes 448 | tf_op jit(solution)/shard_map/squeeze | solution.py:416
  1.4 0.0 copy-start
  1.4 1.2 %copy-done = bf16[1,2,512,512]{3,2,1,0:T(8,128)(2,1)S(1)} copy-done((bf16[1,2,512,512]{3,2,1,0:T(8,128)(2,1)S(1)}, bf16[1,2,512,512]{3,2,1,0:T(8,128)(2,1)}, u32[]{:S(2)}) %copy-start) | copy-done | bytes 1048600
  2.6 0.0 copy-start.4
  2.6 1.0 %copy-done.4 = bf16[4,256,256]{2,1,0:T(8,128)(2,1)S(1)} copy-done((bf16[4,256,256]{2,1,0:T(8,128)(2,1)S(1)}, bf16[4,256,256]{2,1,0:T(8,128)(2,1)}, u32[]{:S(2)}) %copy-start.4) | copy-done | bytes 524312
  3.7 0.0 copy-start.8
  3.7 0.8 %copy-done.8 = bf16[1,2,128,128]{3,2,1,0:T(8,128)(2,1)S(1)} copy-done((bf16[1,2,128,128]{3,2,1,0:T(8,128)(2,1)S(1)}, bf16[1,2,128,128]{3,2,1,0:T(8,128)(2,1)}, u32[]{:S(2)}) %copy-start.8) | copy-done | bytes 65560
  4.5 0.0 copy-start.12
  4.5 0.7 copy-done.12
  5.2 0.0 copy-start.14
  5.2 0.7 copy-done.14
  5.8 5.2 %forward.1 = (f32[14,256,256]{2,1,0:T(8,128)S(1)}, f32[2,14,16,256]{3,2,1,0:T(8,128)S(1)}) custom-call(s32[28,2]{1,0:T(8,128)S(1)} %copy.10.offsets_ref, s32[63]{0:T(128)S(1)} %copy-done.12, s32[28]{0:T(128)S(1)} %copy-done.14, bf16[2,512,512]{2,1,0:T(8,128)(2,1)S(1)} %bitcast.5, bf16[2,128,128]{2,1,0:T(8,128)(2,1)S(1)} %bitcast.7, ...), custom_call_target="tpu_custom_call" | custom-call | tf_op jit(solution)/shard_map/forward/pallas_call | solution.py:246
  11.1 0.0 copy-start.2
  11.1 1.8 %copy-done.2 = f32[14,256,256]{2,1,0:T(8,128)} copy-done((f32[14,256,256]{2,1,0:T(8,128)}, f32[14,256,256]{2,1,0:T(8,128)S(1)}, u32[]{:S(2)}) %copy-start.2) | copy-done | bytes 3670040
  12.8 0.0 copy-start.7
  12.8 0.8 %copy-done.7 = f32[2,14,16,256]{3,2,1,0:T(8,128)} copy-done((f32[2,14,16,256]{3,2,1,0:T(8,128)}, f32[2,14,16,256]{3,2,1,0:T(8,128)S(1)}, u32[]{:S(2)}) %copy-start.7) | copy-done | bytes 458776
  13.6 11.6 %exchange.1 = (f32[2,14,16,256]{3,2,1,0:T(8,128)}, bf16[28,16,128]{2,1,0:T(8,128)(2,1)}, bf16[28,16,128]{2,1,0:T(8,128)(2,1)}) custom-call(f32[2,14,16,256]{3,2,1,0:T(8,128)} %copy-done.7, bf16[28,112,128]{2,1,0:T(8,128)(2,1)} %measured_ref.3), custom_call_target="tpu_custom_call" | custom-call | tf_op jit(solution)/shard_map/exchange/pallas_call | solution.py:319
  25.2 0.0 copy-start.1
  25.2 1.2 %copy-done.1 = bf16[1,2,512,512]{3,2,1,0:T(8,128)(2,1)S(1)} copy-done((bf16[1,2,512,512]{3,2,1,0:T(8,128)(2,1)S(1)}, bf16[1,2,512,512]{3,2,1,0:T(8,128)(2,1)}, u32[]{:S(2)}) %copy-start.1) | copy-done | bytes 1048600
  26.4 0.0 copy-start.3
  26.4 1.1 %copy-done.3 = bf16[28,112,128]{2,1,0:T(8,128)(2,1)S(1)} copy-done((bf16[28,112,128]{2,1,0:T(8,128)(2,1)S(1)}, bf16[28,112,128]{2,1,0:T(8,128)(2,1)}, u32[]{:S(2)}) %copy-start.3) | copy-done | bytes 802840
  27.6 1.0 %copy-done.5 = bf16[4,256,256]{2,1,0:T(8,128)(2,1)S(1)} copy-done((bf16[4,256,256]{2,1,0:T(8,128)(2,1)S(1)}, bf16[4,256,256]{2,1,0:T(8,128)(2,1)}, u32[]{:S(2)}) %copy-start.5) | copy-done | bytes 524312
  28.6 1.0 %copy-done.6 = f32[2,14,16,256]{3,2,1,0:T(8,128)S(1)} copy-done((f32[2,14,16,256]{3,2,1,0:T(8,128)S(1)}, f32[2,14,16,256]{3,2,1,0:T(8,128)}, u32[]{:S(2)}) %copy-start.6) | copy-done | bytes 458776
  29.6 0.8 %copy-done.9 = bf16[1,2,128,128]{3,2,1,0:T(8,128)(2,1)S(1)} copy-done((bf16[1,2,128,128]{3,2,1,0:T(8,128)(2,1)S(1)}, bf16[1,2,128,128]{3,2,1,0:T(8,128)(2,1)}, u32[]{:S(2)}) %copy-start.9) | copy-done | bytes 65560
  30.5 0.9 %copy-done.10 = bf16[28,16,128]{2,1,0:T(8,128)(2,1)S(1)} copy-done((bf16[28,16,128]{2,1,0:T(8,128)(2,1)S(1)}, bf16[28,16,128]{2,1,0:T(8,128)(2,1)}, u32[]{:S(2)}) %copy-start.10) | copy-done | bytes 114712
  31.4 0.9 %copy-done.11 = bf16[28,16,128]{2,1,0:T(8,128)(2,1)S(1)} copy-done((bf16[28,16,128]{2,1,0:T(8,128)(2,1)S(1)}, bf16[28,16,128]{2,1,0:T(8,128)(2,1)}, u32[]{:S(2)}) %copy-start.11) | copy-done | bytes 114712
  32.3 0.7 copy-done.13
  32.9 0.7 copy-done.15
  33.6 6.5 %backward.1 = (f32[4,2,512,128]{3,2,1,0:T(8,128)S(1)}, f32[2,128,128]{2,1,0:T(8,128)S(1)}) custom-call(s32[28,2]{1,0:T(8,128)S(1)} %copy.10.offsets_ref, s32[63]{0:T(128)S(1)} %copy-done.13, s32[28]{0:T(128)S(1)} %copy-done.15, bf16[2,512,512]{2,1,0:T(8,128)(2,1)S(1)} %bitcast.6, bf16[2,128,128]{2,1,0:T(8,128)(2,1)S(1)} %bitcast.8, ...), custom_call_target="tpu_custom_call" | custom-call | tf_op jit(solution)/shard_map/backward/pallas_call | solution.py:270
  40.1 28.3 %reduce_scatter.1 = (f32[2,64,512]{2,1,0:T(8,128)S(1)}, f32[2,16,128]{2,1,0:T(8,128)S(1)}) custom-call(f32[4,2,512,128]{3,2,1,0:T(8,128)S(1)} %get-tuple-element.16.spec_ref, f32[2,128,128]{2,1,0:T(8,128)S(1)} %get-tuple-element.17.pupil_ref), custom_call_target="tpu_custom_call" | custom-call | tf_op jit(solution)/shard_map/reduce_scatter/pallas_call | solution.py:388
  68.4 0.7 %copy.13 = f32[1,2,64,512]{3,2,1,0:T(8,128)} copy(f32[1,2,64,512]{3,2,1,0:T(8,128)S(1)} %bitcast.9) | data formatting | bytes 524288
  69.1 0.6 copy.14
  (7 shorter events, 0.0 us)
Async XLA Ops:
  1.4 1.2 %copy-start = (bf16[1,2,512,512]{3,2,1,0:T(8,128)(2,1)S(1)}, bf16[1,2,512,512]{3,2,1,0:T(8,128)(2,1)}, u32[]{:S(2)}) copy-start(bf16[1,2,512,512]{3,2,1,0:T(8,128)(2,1)} %param.7) | copy-start | bytes 3145732
  2.6 1.0 %copy-start.4 = (bf16[4,256,256]{2,1,0:T(8,128)(2,1)S(1)}, bf16[4,256,256]{2,1,0:T(8,128)(2,1)}, u32[]{:S(2)}) copy-start(bf16[4,256,256]{2,1,0:T(8,128)(2,1)} %constant.2.clone.table_ref) | copy-start | bytes 1572868
  3.7 0.8 %copy-start.8 = (bf16[1,2,128,128]{3,2,1,0:T(8,128)(2,1)S(1)}, bf16[1,2,128,128]{3,2,1,0:T(8,128)(2,1)}, u32[]{:S(2)}) copy-start(bf16[1,2,128,128]{3,2,1,0:T(8,128)(2,1)} %param.8) | copy-start | bytes 196612
  4.5 0.7 copy-start.12
  5.2 0.7 copy-start.14
  11.1 1.8 %copy-start.2 = (f32[14,256,256]{2,1,0:T(8,128)}, f32[14,256,256]{2,1,0:T(8,128)S(1)}, u32[]{:S(2)}) copy-start(f32[14,256,256]{2,1,0:T(8,128)S(1)} %get-tuple-element.15.wave_in) | copy-start | bytes 11010052
  12.8 0.8 %copy-start.7 = (f32[2,14,16,256]{3,2,1,0:T(8,128)}, f32[2,14,16,256]{3,2,1,0:T(8,128)S(1)}, u32[]{:S(2)}) copy-start(f32[2,14,16,256]{3,2,1,0:T(8,128)S(1)} %get-tuple-element.11.edge_ref) | copy-start | bytes 1376260
  25.2 1.2 %copy-start.1 = (bf16[1,2,512,512]{3,2,1,0:T(8,128)(2,1)S(1)}, bf16[1,2,512,512]{3,2,1,0:T(8,128)(2,1)}, u32[]{:S(2)}) copy-start(bf16[1,2,512,512]{3,2,1,0:T(8,128)(2,1)} %param.7) | copy-start | bytes 3145732
  26.4 1.1 %copy-start.3 = (bf16[28,112,128]{2,1,0:T(8,128)(2,1)S(1)}, bf16[28,112,128]{2,1,0:T(8,128)(2,1)}, u32[]{:S(2)}) copy-start(bf16[28,112,128]{2,1,0:T(8,128)(2,1)} %measured_ref.3) | copy-start | bytes 2408452
  27.6 1.0 %copy-start.5 = (bf16[4,256,256]{2,1,0:T(8,128)(2,1)S(1)}, bf16[4,256,256]{2,1,0:T(8,128)(2,1)}, u32[]{:S(2)}) copy-start(bf16[4,256,256]{2,1,0:T(8,128)(2,1)} %constant.2.clone.table_ref) | copy-start | bytes 1572868
  28.6 1.0 %copy-start.6 = (f32[2,14,16,256]{3,2,1,0:T(8,128)S(1)}, f32[2,14,16,256]{3,2,1,0:T(8,128)}, u32[]{:S(2)}) copy-start(f32[2,14,16,256]{3,2,1,0:T(8,128)} %get-tuple-element.14.edge_ref) | copy-start | bytes 1376260
  29.6 0.8 %copy-start.9 = (bf16[1,2,128,128]{3,2,1,0:T(8,128)(2,1)S(1)}, bf16[1,2,128,128]{3,2,1,0:T(8,128)(2,1)}, u32[]{:S(2)}) copy-start(bf16[1,2,128,128]{3,2,1,0:T(8,128)(2,1)} %param.8) | copy-start | bytes 196612
  30.5 0.9 %copy-start.10 = (bf16[28,16,128]{2,1,0:T(8,128)(2,1)S(1)}, bf16[28,16,128]{2,1,0:T(8,128)(2,1)}, u32[]{:S(2)}) copy-start(bf16[28,16,128]{2,1,0:T(8,128)(2,1)} %get-tuple-element.12.above_ref) | copy-start | bytes 344068
  31.4 0.9 %copy-start.11 = (bf16[28,16,128]{2,1,0:T(8,128)(2,1)S(1)}, bf16[28,16,128]{2,1,0:T(8,128)(2,1)}, u32[]{:S(2)}) copy-start(bf16[28,16,128]{2,1,0:T(8,128)(2,1)} %get-tuple-element.13.below_ref) | copy-start | bytes 344068
  32.3 0.7 copy-start.13
  32.9 0.7 copy-start.15

commit v2 on v1

v2 whole, which is shorter than its diff:
```python
from functools import partial
import math

import jax
import jax.numpy as jnp
import ml_dtypes
import numpy as np
from jax import lax
from jax.experimental import pallas as pl
from jax.experimental.pallas import tpu as pltpu
from jax.sharding import PartitionSpec as P

PUP = 128
OV = 16
HALF = 8
STRIDE = PUP - OV
BLOCKS = 4
MESH = pl.DeviceIdType.MESH
F32 = jnp.float32
BF16 = jnp.bfloat16
XS, YS = 4, 2
SPEC_ROWS = 512 // (XS * YS)
PUP_ROWS = PUP // (XS * YS)
ROWS_B = 4 * SPEC_ROWS
ROWS_A = ROWS_B + 2 * PUP_ROWS
LEVELS = 32767.0
PAIRS = 2
GROUP = 2 * PAIRS
VMEM_LIMIT = 63 * 1024 * 1024
GATHER_LIMIT = 62 * 1024 * 1024


def dft_tables():
    k = np.arange(PUP)
    angle = 2.0 * np.pi * ((k[:, None] * k[None, :]) % PUP) / PUP
    cosine, sine = np.cos(angle), np.sin(angle)
    inverse = np.block([[cosine, sine], [-sine, cosine]]) / PUP
    forward = np.block([[cosine, -sine], [sine, cosine]])
    parts = []
    for table in (inverse, forward):
        high = table.astype(ml_dtypes.bfloat16)
        low = (table - high.astype(np.float64)).astype(ml_dtypes.bfloat16)
        parts += [high, low]
    return np.stack(parts)


def split(x):
    high = x.astype(BF16)
    return high, (x - high.astype(F32)).astype(BF16)


def right_product(x, high, low):
    xh, xl = split(x)
    data = jnp.concatenate([xh, xl, xh], axis=1)
    table = jnp.concatenate([high, high, low], axis=0)
    return jnp.dot(data, table, preferred_element_type=F32)


def left_product(high, low, x):
    xh, xl = split(x)
    data = jnp.concatenate([xh, xl, xh], axis=0)
    table = jnp.concatenate([high, high, low], axis=1)
    return jnp.dot(table, data, preferred_element_type=F32)


def swap_blocks(x):
    top = jnp.concatenate([x[:PUP, :PUP], x[PUP:, :PUP]], axis=1)
    bottom = jnp.concatenate([x[:PUP, PUP:], x[PUP:, PUP:]], axis=1)
    return jnp.concatenate([top, bottom], axis=0)


def ramp_weights(widths_ref, tile, tiles):
    place = lax.broadcasted_iota(jnp.int32, (OV, PUP), 0).astype(F32)
    above = widths_ref[jnp.maximum(tile - 1, 0)].astype(F32)
    below = widths_ref[jnp.minimum(tile, tiles - 2)].astype(F32)
    top = 1.0 - jnp.clip(0.5 + (HALF - 0.5 - place) / above, 0.0, 1.0)
    bottom = jnp.clip(0.5 + (HALF - 0.5 - place) / below, 0.0, 1.0)
    ones = jnp.ones_like(place)
    return jnp.where(tile > 0, top, ones), jnp.where(tile < tiles - 1, bottom, ones)


def list_live(live_ref, order_ref):
    def body(led, count):
        order_ref[count] = led
        return count + live_ref[led]

    lamps = live_ref.shape[0]
    count = lax.fori_loop(0, lamps, body, jnp.int32(0))
    for extra in range(GROUP):
        order_ref[count + extra] = 0
    return count


def load_spectrum(spec_ref, planes):
    for block in range(BLOCKS):
        for part in range(2):
            planes[block, part] = spec_ref[part, :, block * PUP : (block + 1) * PUP].astype(F32)


def window_of(planes, row, col):
    first = col // PUP
    second = jnp.minimum(first + 1, BLOCKS - 1)
    lanes = lax.broadcasted_iota(jnp.int32, (PUP, PUP), 1)
    inside = lanes >= col % PUP
    return [
        jnp.where(inside, planes[first, part, pl.ds(row, PUP), :], planes[second, part, pl.ds(row, PUP), :])
        for part in range(2)
    ]


def forward_kernel(
    offsets_hbm, widths_hbm, spec_hbm, pupil_hbm, table_hbm, measured_hbm,
    wave_out, near, above, below,
    waves, edges, planes, offsets_ref, widths_ref, spec_ref, pupil_ref, table_ref,
    local_sems, wave_sems, send_sems, recv_sems, image_send, image_recv
):
    tiles = lax.axis_size("tile")
    tile = lax.axis_index("tile")
    up, down = lax.rem(tile + tiles - 1, tiles), lax.rem(tile + 1, tiles)
    steps = waves.shape[0] // GROUP
    local = [
        pltpu.make_async_copy(source, target, local_sems.at[number])
        for number, (source, target) in enumerate(
            (
                (offsets_hbm, offsets_ref),
                (widths_hbm, widths_ref),
                (spec_hbm, spec_ref),
                (pupil_hbm, pupil_ref),
                (table_hbm, table_ref),
            )
        )
    ]
    for copy in local:
        copy.start()
    barrier = pltpu.get_barrier_semaphore()
    for other in (up, down):
        pl.semaphore_signal(barrier, inc=1, device_id={"tile": other}, device_id_type=MESH)
    for copy in local[:3]:
        copy.wait()
    load_spectrum(spec_ref, planes)
    top, bottom = ramp_weights(widths_ref, tile, tiles)
    top2 = jnp.concatenate([top, top], axis=1)
    bottom2 = jnp.concatenate([bottom, bottom], axis=1)
    for copy in local[3:]:
        copy.wait()
    pl.semaphore_wait(barrier, 2)

    def remote(source, target, send_sem, recv_sem, other):
        return pltpu.make_async_remote_copy(
            src_ref=source, dst_ref=target, send_sem=send_sem, recv_sem=recv_sem,
            device_id={"tile": other}, device_id_type=MESH,
        )

    images = [
        remote(measured_hbm.at[:, pl.ds(0, OV)], below, image_send.at[0], image_recv.at[0], up),
        remote(measured_hbm.at[:, pl.ds(STRIDE - OV, OV)], above, image_send.at[1], image_recv.at[1], down),
    ]
    for copy in images:
        copy.start()

    def edge_copies(number):
        here = pl.ds(number * GROUP, GROUP)
        return [
            remote(edges.at[end, here], near.at[end, here], send_sems.at[end, number], recv_sems.at[end, number], other)
            for end, other in ((0, up), (1, down))
        ]

    def wave_copy(number):
        here = pl.ds(number * GROUP, GROUP)
        return pltpu.make_async_copy(waves.at[here], wave_out.at[here], wave_sems.at[number])

    def field_of(led):
        row, col = offsets_ref[0, led], offsets_ref[1, led]
        win_re, win_im = window_of(planes, row, col)
        shift = col % PUP
        pup_re = pltpu.roll(pupil_ref[0].astype(F32), shift, axis=1)
        pup_im = pltpu.roll(pupil_ref[1].astype(F32), shift, axis=1)
        return jnp.concatenate(
            [pup_re * win_re - pup_im * win_im, pup_re * win_im + pup_im * win_re], axis=1
        )

    def step(number, carry):
        for inner in range(PAIRS):
            pair = number * PAIRS + inner
            field = jnp.concatenate([field_of(2 * pair), field_of(2 * pair + 1)], axis=0)
            mixed = right_product(field, table_ref[0], table_ref[1])
            wave = left_product(table_ref[2], table_ref[3], swap_blocks(mixed))
            first = wave[:OV], wave[PUP : PUP + OV]
            last = wave[STRIDE:PUP], wave[PUP + STRIDE :]
            first = (top2 * (first[0] * first[0] + first[1] * first[1])).astype(BF16)
            last = (bottom2 * (last[0] * last[0] + last[1] * last[1])).astype(BF16)
            for side in range(2):
                lo = side * PUP
                led = 2 * pair + side
                waves[led] = wave[:, lo : lo + PUP]
                edges[0, led] = first[:, lo : lo + PUP]
                edges[1, led] = last[:, lo : lo + PUP]
        wave_copy(number).start()
        for copy in edge_copies(number):
            copy.start()
        return carry

    lax.fori_loop(0, steps, step, 0)

    def finish(number, carry):
        wave_copy(number).wait()
        for copy in edge_copies(number):
            copy.wait()
        return carry

    lax.fori_loop(0, steps, finish, 0)
    for copy in images:
        copy.wait()


def my_place():
    me = lax.axis_index("led")
    return me // XS, me % XS


def dest_of(line, place):
    return (line % YS) * XS + place % XS


def backward_kernel(
    scale, offsets_hbm, widths_hbm, live_hbm, spec_hbm, pupil_hbm, table_hbm, measured_hbm, above_hbm, below_hbm, edge_hbm, wave_hbm,
    codes_a_hbm, scales_a_hbm, own_a_hbm, codes_b_hbm, scales_b_hbm, own_b_hbm,
    spec_out, pupil_out, codes_a, scales_a, own_a, codes_b, scales_b, own_b, waves, planes, offsets_ref, widths_ref, live_ref, order_ref, spec_ref, pupil_ref, table_ref, measured_ref,
    above_ref, below_ref, edge_ref, sems, wave_sems, out_sems
):
    tiles = lax.axis_size("tile")
    tile = lax.axis_index("tile")
    local = [
        pltpu.make_async_copy(source, target, sems.at[number])
        for number, (source, target) in enumerate(
            (
                (offsets_hbm, offsets_ref),
                (widths_hbm, widths_ref),
                (live_hbm, live_ref),
                (spec_hbm, spec_ref),
                (pupil_hbm, pupil_ref),
                (table_hbm, table_ref),
                (measured_hbm, measured_ref),
                (above_hbm, above_ref),
                (below_hbm, below_ref),
                (edge_hbm, edge_ref),
            )
        )
    ]
    for copy in local:
        copy.start()

    for copy in local[:3]:
        copy.wait()
    count = list_live(live_ref, order_ref)
    steps = (count + GROUP - 1) // GROUP

    def wave_copy(slot):
        return pltpu.make_async_copy(wave_hbm.at[order_ref[slot]], waves.at[slot], wave_sems.at[slot])

    def fetch(slot, carry):
        wave_copy(slot).start()
        return carry

    lax.fori_loop(0, steps * GROUP, fetch, 0)

    spec_out[...] = jnp.zeros_like(spec_out)
    pupil_out[...] = jnp.zeros_like(pupil_out)
    local[3].wait()
    load_spectrum(spec_ref, planes)
    for copy in local[4:]:
        copy.wait()
    top, bottom = ramp_weights(widths_ref, tile, tiles)
    top2 = jnp.concatenate([top, top], axis=1)
    bottom2 = jnp.concatenate([bottom, bottom], axis=1)
    rows = lax.broadcasted_iota(jnp.int32, (OV, 2 * PUP), 0)
    top_grad = jnp.where((tile > 0) | (rows >= HALF), 2.0 * top2, 0.0)
    bottom_grad = jnp.where((tile < tiles - 1) | (rows < HALF), 2.0 * bottom2, 0.0)
    has_above = tile > 0
    has_below = tile < tiles - 1
    lanes = lax.broadcasted_iota(jnp.int32, (PUP, PUP), 1)

    def edges_of(end, leds):
        return jnp.concatenate([edge_ref[end, led].astype(F32) for led in leds], axis=1)

    def images(ref, leds, low, high):
        return jnp.concatenate([ref[led, low:high].astype(F32) for led in leds], axis=1)

    def step(number, carry):
        for inner in range(GROUP):
            wave_copy(number * GROUP + inner).wait()
        for inner in range(PAIRS):
            pair = number * PAIRS + inner
            leds = order_ref[2 * pair], order_ref[2 * pair + 1]
            side_of = lax.broadcasted_iota(jnp.int32, (1, 2 * PUP), 1) // PUP
            alive = jnp.where(2 * pair + side_of < count, scale, 0.0)
            wave = jnp.concatenate([waves[2 * pair], waves[2 * pair + 1]], axis=1)
            wave_re, wave_im = wave[:PUP], wave[PUP:]
            intensity = wave_re * wave_re + wave_im * wave_im
            own = images(measured_ref, leds, 0, STRIDE)
            upper = images(above_ref, leds, OV - HALF, OV)
            lower = images(below_ref, leds, 0, HALF)
            near_top = jnp.where(has_above, edges_of(1, leds), 0.0)
            near_bottom = jnp.where(has_below, edges_of(0, leds), 0.0)
            first = top_grad * (top2 * intensity[:OV] + near_top - jnp.concatenate([upper, own[: OV - HALF]], axis=0))
            middle = 2.0 * (intensity[OV:STRIDE] - own[HALF : STRIDE - HALF])
            last = bottom_grad * (bottom2 * intensity[STRIDE:] + near_bottom - jnp.concatenate([own[STRIDE - HALF :], lower], axis=0))
            grad = alive * jnp.concatenate([first, middle, last], axis=0)
            grad_wave = jnp.concatenate([grad * wave_re, grad * wave_im], axis=0)
            back = right_product(swap_blocks(grad_wave), table_ref[2], table_ref[3])
            grad_field = left_product(table_ref[0], table_ref[1], swap_blocks(back))
            for side in range(2):
                led = leds[side]
                row, col = offsets_ref[0, led], offsets_ref[1, led]
                shift = col % PUP
                lo = side * PUP
                grad_re = grad_field[:PUP, lo : lo + PUP]
                grad_im = grad_field[PUP:, lo : lo + PUP]
                pup_re = pltpu.roll(pupil_ref[0].astype(F32), shift, axis=1)
                pup_im = pltpu.roll(pupil_ref[1].astype(F32), shift, axis=1)
                win_re, win_im = window_of(planes, row, col)
                pieces = (pup_re * grad_re + pup_im * grad_im, pup_re * grad_im - pup_im * grad_re)
                shares = (win_re * grad_re + win_im * grad_im, win_re * grad_im - win_im * grad_re)
                first_block = col // PUP
                second_block = jnp.minimum(first_block + 1, BLOCKS - 1)
                inside = lanes >= shift
                for part in range(2):
                    here_rows = pl.ds(row, PUP)
                    pupil_out[part] += pltpu.roll(shares[part], PUP - shift, axis=1)
                    spec_out[first_block, part, here_rows, :] += jnp.where(inside, pieces[part], 0.0)
                    spec_out[second_block, part, here_rows, :] += jnp.where(inside, 0.0, pieces[part])
        return carry

    lax.fori_loop(0, steps, step, 0)
    line, place = my_place()
    depth = SPEC_ROWS
    sends = []

    def keep(source, target):
        sends.append(pltpu.make_async_copy(source, target, out_sems.at[len(sends)]))
        sends[-1].start()

    def pieces_of(half, dest):
        rows = pl.ds(pl.multiple_of(dest * depth, depth), depth)
        pieces = [spec_out[2 * half + block, part, rows, :] for block in range(2) for part in range(2)]
        if half == 0:
            width = PUP_ROWS
            rows = pl.ds(pl.multiple_of(dest * width, width), width)
            pieces += [pupil_out[part, rows, :] for part in range(2)]
        return pieces

    def encode(pieces, codes, scales):
        start = 0
        for number, piece in enumerate(pieces):
            most = jnp.maximum(jnp.max(jnp.abs(piece), axis=0, keepdims=True), 1e-30)
            stop = start + piece.shape[0]
            codes[start:stop, :] = jnp.round(piece * (LEVELS / most)).astype(jnp.int16)
            scales[number : number + 1, :] = most * (1.0 / LEVELS)
            start = stop

    def store(pieces, target):
        start = 0
        for piece in pieces:
            stop = start + piece.shape[0]
            target[start:stop, :] = piece
            start = stop

    for hop in range(XS):
        encode(pieces_of(1, dest_of(line + 1, place + 1 + hop)), codes_b.at[hop], scales_b.at[hop])
        keep(codes_b.at[hop], codes_b_hbm.at[hop])
    for turn in range(2):
        for hop in range(XS - 1):
            encode(pieces_of(0, dest_of(line + 1 + turn, place + 1 + hop)), codes_a.at[turn, hop], scales_a.at[turn, hop])
            keep(codes_a.at[turn, hop], codes_a_hbm.at[turn, hop])
        store(pieces_of(0, dest_of(line + 1 + turn, place)), own_a.at[turn])
    for hop in range(XS):
        store(pieces_of(1, dest_of(line, place + 1 + hop)), own_b.at[hop])
    keep(scales_a, scales_a_hbm)
    keep(scales_b, scales_b_hbm)
    keep(own_a, own_a_hbm)
    keep(own_b, own_b_hbm)
    for copy in sends:
        copy.wait()


def vmem():
    return pl.BlockSpec(memory_space=pltpu.VMEM)


def smem():
    return pl.BlockSpec(memory_space=pltpu.SMEM)


def hbm():
    return pl.BlockSpec(memory_space=pltpu.HBM)


def shape(dims, dtype):
    return jax.ShapeDtypeStruct(dims, dtype)


def forward_call(offsets, widths, spectrum, pupil, tables, measured):
    lamps = measured.shape[0]
    side = spectrum.shape[-1]
    rows = shape((lamps, OV, PUP), measured.dtype)
    wave = (lamps, 2 * PUP, PUP)
    edge = (2, lamps, OV, PUP)
    chunks = lamps // GROUP
    return pl.pallas_call(
        forward_kernel,
        out_shape=(shape(wave, F32), shape(edge, BF16), rows, rows),
        in_specs=[hbm()] * 6,
        out_specs=(hbm(),) * 4,
        scratch_shapes=[
            pltpu.VMEM(wave, F32),
            pltpu.VMEM(edge, BF16),
            pltpu.VMEM((BLOCKS, 2, side, PUP), F32),
            pltpu.SMEM(offsets.shape, jnp.int32),
            pltpu.SMEM(widths.shape, jnp.int32),
            pltpu.VMEM(spectrum.shape, spectrum.dtype),
            pltpu.VMEM(pupil.shape, pupil.dtype),
            pltpu.VMEM(tables.shape, tables.dtype),
            pltpu.SemaphoreType.DMA((5,)),
            pltpu.SemaphoreType.DMA((chunks,)),
            pltpu.SemaphoreType.DMA((2, chunks)),
            pltpu.SemaphoreType.DMA((2, chunks)),
            pltpu.SemaphoreType.DMA((2,)),
            pltpu.SemaphoreType.DMA((2,)),
        ],
        compiler_params=pltpu.CompilerParams(
            collective_id=1, has_side_effects=True, vmem_limit_bytes=VMEM_LIMIT
        ),
        name="forward",
    )(offsets, widths, spectrum, pupil, tables, measured)


UNITS = (
    ((2, XS - 1, ROWS_A, PUP), jnp.int16),
    ((2, XS - 1, 8, PUP), F32),
    ((2, ROWS_A, PUP), F32),
    ((XS, ROWS_B, PUP), jnp.int16),
    ((XS, 8, PUP), F32),
    ((XS, ROWS_B, PUP), F32),
)


def backward_call(scale, offsets, widths, live, spectrum, pupil, tables, measured, above, below, edges, waves):
    lamps = measured.shape[0]
    side = spectrum.shape[-1]
    planes = pltpu.VMEM((BLOCKS, 2, side, PUP), F32)
    return pl.pallas_call(
        partial(backward_kernel, scale),
        out_shape=tuple(shape(*unit) for unit in UNITS),
        in_specs=[hbm()] * 11,
        out_specs=(hbm(),) * 6,
        scratch_shapes=[
            planes,
            pltpu.VMEM(pupil.shape, F32),
            *(pltpu.VMEM(*unit) for unit in UNITS),
            pltpu.VMEM(waves.shape, F32),
            planes,
            pltpu.SMEM(offsets.shape, jnp.int32),
            pltpu.SMEM(widths.shape, jnp.int32),
            pltpu.SMEM(live.shape, jnp.int32),
            pltpu.SMEM((lamps + GROUP,), jnp.int32),
            pltpu.VMEM(spectrum.shape, spectrum.dtype),
            pltpu.VMEM(pupil.shape, pupil.dtype),
            pltpu.VMEM(tables.shape, tables.dtype),
            pltpu.VMEM(measured.shape, measured.dtype),
            pltpu.VMEM(above.shape, above.dtype),
            pltpu.VMEM(below.shape, below.dtype),
            pltpu.VMEM(edges.shape, edges.dtype),
            pltpu.SemaphoreType.DMA((10,)),
            pltpu.SemaphoreType.DMA((lamps,)),
            pltpu.SemaphoreType.DMA((14,)),
        ],
        compiler_params=pltpu.CompilerParams(vmem_limit_bytes=VMEM_LIMIT),
        name="backward",
    )(offsets, widths, live, spectrum, pupil, tables, measured, above, below, edges, waves)


def gather_kernel(
    codes_a, scales_a, own_a_hbm, codes_b, scales_b, own_b_hbm, spec_out, pupil_out,
    own_a, own_b, held_a, held_scales_a, held_b, held_scales_b, code_a2, scale_a2, held_a2, held_scales_a2,
    codes_b2, scales_b2, held_b2, held_scales_b2, local_sems, send_sems, recv_sems
):
    line, place = my_place()
    local = [
        pltpu.make_async_copy(own_a_hbm, own_a, local_sems.at[0]),
        pltpu.make_async_copy(own_b_hbm, own_b, local_sems.at[1]),
    ]
    for copy in local:
        copy.start()
    opposite = dest_of(line + 1, place)
    beside = [dest_of(line, place + 1 + hop) for hop in range(XS - 1)]
    barrier = pltpu.get_barrier_semaphore()
    for other in [opposite, *beside]:
        pl.semaphore_signal(barrier, inc=1, device_id={"led": other}, device_id_type=MESH)
    pl.semaphore_wait(barrier, XS)
    used = [0]

    def send(source, target, scale_source, scale_target, other):
        pair = []
        for src, dst in ((source, target), (scale_source, scale_target)):
            number = used[0]
            used[0] += 1
            pair.append(
                pltpu.make_async_remote_copy(
                    src_ref=src, dst_ref=dst, send_sem=send_sems.at[number], recv_sem=recv_sems.at[number],
                    device_id={"led": other}, device_id_type=MESH,
                )
            )
            pair[-1].start()
        return pair

    first_a = [[None] * (XS - 1), [None] * (XS - 1)]
    first_b = [None] * XS
    for hop in range(XS):
        first_b[hop] = send(codes_b.at[hop], held_b.at[hop], scales_b.at[hop], held_scales_b.at[hop], opposite)
        if hop < XS - 1:
            first_a[0][hop] = send(
                codes_a.at[0, hop], held_a.at[0, hop], scales_a.at[0, hop], held_scales_a.at[0, hop], beside[hop]
            )
    for hop in range(XS - 1):
        first_a[1][hop] = send(
            codes_a.at[1, hop], held_a.at[1, hop], scales_a.at[1, hop], held_scales_a.at[1, hop], beside[hop]
        )
    for copy in local:
        copy.wait()

    def arrived(pair):
        for copy in pair:
            copy.wait()

    bounds_b = [(number * SPEC_ROWS, (number + 1) * SPEC_ROWS) for number in range(4)]
    bounds_a = bounds_b + [(ROWS_B + part * PUP_ROWS, ROWS_B + (part + 1) * PUP_ROWS) for part in range(2)]

    def total(own, parts, number, start, stop):
        value = own[start:stop, :]
        for codes, scales in parts:
            value += codes[start:stop, :].astype(F32) * scales[number : number + 1, :]
        return value

    def encode(own, parts, bounds, codes, scales):
        for number, (start, stop) in enumerate(bounds):
            value = total(own, parts, number, start, stop)
            most = jnp.maximum(jnp.max(jnp.abs(value), axis=0, keepdims=True), 1e-30)
            codes[start:stop, :] = jnp.round(value * (LEVELS / most)).astype(jnp.int16)
            scales[number : number + 1, :] = most * (1.0 / LEVELS)

    second_b = [None] * (XS - 1)

    def pass_on(hop):
        arrived(first_b[hop])
        parts = [(held_b.at[hop], held_scales_b.at[hop])]
        encode(own_b.at[hop], parts, bounds_b, codes_b2.at[hop], scales_b2.at[hop])
        second_b[hop] = send(codes_b2.at[hop], held_b2.at[hop], scales_b2.at[hop], held_scales_b2.at[hop], beside[hop])

    pass_on(0)
    pass_on(1)
    for hop in range(XS - 1):
        arrived(first_a[0][hop])
    parts = [(held_a.at[0, hop], held_scales_a.at[0, hop]) for hop in range(XS - 1)]
    encode(own_a.at[0], parts, bounds_a, code_a2, scale_a2)
    second_a = send(code_a2, held_a2, scale_a2, held_scales_a2, opposite)
    pass_on(2)
    for hop in range(XS - 1):
        arrived(first_a[1][hop])
    arrived(second_a)
    parts = [(held_a.at[1, hop], held_scales_a.at[1, hop]) for hop in range(XS - 1)] + [(held_a2, held_scales_a2)]
    for number, (start, stop) in enumerate(bounds_a):
        value = total(own_a.at[1], parts, number, start, stop)
        if number < 4:
            block, part = number // 2, number % 2
            spec_out[part, :, block * PUP : (block + 1) * PUP] = value
        else:
            pupil_out[number - 4] = value
    arrived(first_b[XS - 1])
    for hop in range(XS - 1):
        arrived(second_b[hop])
    parts = [(held_b.at[XS - 1], held_scales_b.at[XS - 1])]
    parts += [(held_b2.at[hop], held_scales_b2.at[hop]) for hop in range(XS - 1)]
    for number, (start, stop) in enumerate(bounds_b):
        block, part = 2 + number // 2, number % 2
        spec_out[part, :, block * PUP : (block + 1) * PUP] = total(own_b.at[XS - 1], parts, number, start, stop)


def gather_call(codes_a, scales_a, own_a, codes_b, scales_b, own_b):
    moved = 2 * (2 * (XS - 1) + XS + 1 + XS - 1)
    code2 = pltpu.VMEM((ROWS_A, PUP), jnp.int16)
    scale2 = pltpu.VMEM((8, PUP), F32)
    codes2 = pltpu.VMEM((XS - 1, ROWS_B, PUP), jnp.int16)
    scales2 = pltpu.VMEM((XS - 1, 8, PUP), F32)
    return pl.pallas_call(
        gather_kernel,
        out_shape=(shape((2, SPEC_ROWS, BLOCKS * PUP), F32), shape((2, PUP_ROWS, PUP), F32)),
        in_specs=[hbm()] * 6,
        out_specs=(vmem(), vmem()),
        scratch_shapes=[
            pltpu.VMEM(own_a.shape, F32),
            pltpu.VMEM(own_b.shape, F32),
            pltpu.VMEM(codes_a.shape, codes_a.dtype),
            pltpu.VMEM(scales_a.shape, F32),
            pltpu.VMEM(codes_b.shape, codes_b.dtype),
            pltpu.VMEM(scales_b.shape, F32),
            code2,
            scale2,
            code2,
            scale2,
            codes2,
            scales2,
            codes2,
            scales2,
            pltpu.SemaphoreType.DMA((2,)),
            pltpu.SemaphoreType.DMA((moved,)),
            pltpu.SemaphoreType.DMA((moved,)),
        ],
        compiler_params=pltpu.CompilerParams(
            collective_id=2, has_side_effects=True, vmem_limit_bytes=GATHER_LIMIT
        ),
        name="reduce_scatter",
    )(codes_a, scales_a, own_a, codes_b, scales_b, own_b)


def on_device(tables, spectrum, pupil, offsets, widths, live, measured):
    groups = lax.axis_size("led")
    lamps = measured.shape[0]
    scale = 1.0 / math.sqrt(lamps * groups)
    spectrum, pupil, offsets = spectrum[0], pupil[0], offsets[0].T
    waves, near, above, below = forward_call(offsets, widths, spectrum, pupil, tables, measured)
    parts = backward_call(
        scale, offsets, widths, live, spectrum, pupil, tables, measured, above, below, near, waves
    )
    spec_share, pupil_share = gather_call(*parts)
    return spec_share[None], pupil_share[None]


def solution(mesh):
    tables = dft_tables()

    def run(spectrum, pupil, offsets, widths, live, measured):
        return jax.shard_map(
            on_device,
            mesh=mesh,
            in_specs=(
                P(),
                P("tile", None, None, None),
                P("tile", None, None, None),
                P("tile", "led", None),
                P(),
                P("led"),
                P("led", "tile", None),
            ),
            out_specs=(P("tile", None, "led", None), P("tile", None, "led", None)),
            check_vma=False,
        )(jnp.asarray(tables), spectrum, pupil, offsets, widths, live, measured)

    return run
```

time: 70.3 us -> 50.8 us (0.72)
  the two profiles are of different devices: /device:TPU:257 before, /device:TPU:2 now
where the time goes in v2:
time: 50.8 us; the launch traced here: 50.5 us
  Pallas kernels  46.9 us (92%)
  local copies, waits for them, and re-layouts  2.99 us (6%)
  between operations  0.65 us (1%)
    pallas_call x1, Pallas kernels, forward_call(): pl.pallas_call(forward_kernel, out_shape=(shape(wave, F32), shape(edge, B...  20.7 us
    pallas_call x1, Pallas kernels, gather_call(): pl.pallas_call(gather_kernel, out_shape=(shape((2, SPEC_ROWS, BLOCKS * PU...  16.7 us
    pallas_call x1, Pallas kernels, backward_call(): pl.pallas_call(partial(backward_kernel, scale), out_shape=tuple((shape(*u...  9.53 us
    unnamed x2, local copies, waits for them, and re-layouts  2.99 us

profile of v2, /device:TPU:2, one launch (start us, length us, event | category | flops | bytes accessed | tf_op | source)
XLA Modules:
  0.0 50.5 jit_solution(5571947723048727742)
XLA Ops:
  0.6 20.7 %forward.1 = (f32[28,256,128]{2,1,0:T(8,128)}, bf16[2,28,16,128]{3,2,1,0:T(8,128)(2,1)}, bf16[28,16,128]{2,1,0:T(8,128)(2,1)}, bf16[28,16,128]{2,1,0:T(8,128)(2,1)}) custom-call(s32[2,28]{1,0:T(2,128)} %bitcast.13, s32[63]{0:T(128)} %widths_hbm.3, bf16[2,512,512]{2,1,0:T(8,128)(2,1)} %bitcast.7, bf16[2,128,128]{2,1,0:T(8,128)(2,1)} %bitcast.9, ...), custom_call_target="tpu_custom_call" | custom-call | tf_op jit(solution)/shard_map/forward/pallas_call | solution.py:409
  21.3 9.5 %backward.1 = (s16[2,3,288,128]{3,2,1,0:T(8,128)(2,1)}, f32[2,3,8,128]{3,2,1,0:T(8,128)}, f32[2,288,128]{2,1,0:T(8,128)}, s16[4,256,128]{2,1,0:T(8,128)(2,1)}, f...) custom-call(s32[2,28]{1,0:T(2,128)} %bitcast.14, s32[63]{0:T(128)} %widths_hbm.3, s32[28]{0:T(128)} %live_hbm.1, ...), custom_call_target="tpu_custom_call" | custom-call | tf_op jit(solution)/shard_map/backward/pallas_call | solution.py:451
  30.8 16.7 %reduce_scatter.1 = (f32[2,64,512]{2,1,0:T(8,128)}, f32[2,16,128]{2,1,0:T(8,128)}) custom-call(s16[2,3,288,128]{3,2,1,0:T(8,128)(2,1)} %get-tuple-element.18.codes_a, f32[2,3,8,128]{3,2,1,0:T(8,128)} %get-tuple-element.19.scales_a, f32[2,288,128]{2,1,0:T(8,128)} %get-tuple-element.20.own_a_hbm, s16[4,256,128]{2,1,0:T(8,128)(2,1)} %get-tuple-element.21.codes_b, ...), custom_call_target="tpu_custom_call" | custom-call | tf_op jit(solution)/shard_map/reduce_scatter/pallas_call | solution.py:594
  47.6 1.7 %copy.11 = f32[1,2,64,512]{3,2,1,0:T(8,128)} copy(f32[1,2,64,512]{3,2,1,0:T(8,128)} %bitcast.11) | data formatting | bytes 524288
  49.2 1.3 %copy.12 = f32[1,2,16,128]{3,2,1,0:T(8,128)} copy(f32[1,2,16,128]{3,2,1,0:T(8,128)} %bitcast.12) | data formatting | bytes 32768

commit v3 on v2

--- a/solution.py
+++ b/solution.py
@@ -21,13 +21,23 @@
 XS, YS = 4, 2
 SPEC_ROWS = 512 // (XS * YS)
 PUP_ROWS = PUP // (XS * YS)
-ROWS_B = 4 * SPEC_ROWS
-ROWS_A = ROWS_B + 2 * PUP_ROWS
+CHUNKS = [(block, part) for block in range(BLOCKS) for part in range(2)]
+CHUNKS_A, CHUNKS_B = CHUNKS[:3], CHUNKS[3:]
+BOUNDS_B = [(number * SPEC_ROWS, (number + 1) * SPEC_ROWS) for number in range(len(CHUNKS_B))]
+ROWS_B = len(CHUNKS_B) * SPEC_ROWS
+BOUNDS_A = BOUNDS_B[: len(CHUNKS_A)]
+BOUNDS_A += [(len(CHUNKS_A) * SPEC_ROWS + part * PUP_ROWS, len(CHUNKS_A) * SPEC_ROWS + (part + 1) * PUP_ROWS) for part in range(2)]
+ROWS_A = len(CHUNKS_A) * SPEC_ROWS + 2 * PUP_ROWS
+SENT_A, SENT_B = 2 * (XS - 1), XS
+CODE_ROWS = SENT_A * ROWS_A + SENT_B * ROWS_B
+OWN_ROWS = 2 * ROWS_A + SENT_B * ROWS_B
+FLOAT_ROWS = OWN_ROWS + 8 * (SENT_A + SENT_B)
 LEVELS = 32767.0
-PAIRS = 2
+FORWARD_PAIRS = 7
+PAIRS = 4
 GROUP = 2 * PAIRS
 VMEM_LIMIT = 63 * 1024 * 1024
-GATHER_LIMIT = 62 * 1024 * 1024
+GATHER_LIMIT = 213 * 256 * 1024
 
 
 def dft_tables():
@@ -116,8 +126,9 @@
 ):
     tiles = lax.axis_size("tile")
     tile = lax.axis_index("tile")
-    up, down = lax.rem(tile + tiles - 1, tiles), lax.rem(tile + 1, tiles)
-    steps = waves.shape[0] // GROUP
+    up, down = jnp.maximum(tile - 1, 0), jnp.minimum(tile + 1, tiles - 1)
+    width = 2 * FORWARD_PAIRS
+    steps = waves.shape[0] // width
     local = [
         pltpu.make_async_copy(source, target, local_sems.at[number])
         for number, (source, target) in enumerate(
@@ -133,8 +144,13 @@
     for copy in local:
         copy.start()
     barrier = pltpu.get_barrier_semaphore()
-    for other in (up, down):
+    has_above, has_below = tile > 0, tile < tiles - 1
+
+    def signal(other):
         pl.semaphore_signal(barrier, inc=1, device_id={"tile": other}, device_id_type=MESH)
+
+    pl.when(has_above)(lambda: signal(up))
+    pl.when(has_below)(lambda: signal(down))
     for copy in local[:3]:
         copy.wait()
     load_spectrum(spec_ref, planes)
@@ -143,7 +159,7 @@
     bottom2 = jnp.concatenate([bottom, bottom], axis=1)
     for copy in local[3:]:
         copy.wait()
-    pl.semaphore_wait(barrier, 2)
+    pl.semaphore_wait(barrier, has_above.astype(jnp.int32) + has_below.astype(jnp.int32))
 
     def remote(source, target, send_sem, recv_sem, other):
         return pltpu.make_async_remote_copy(
@@ -151,22 +167,22 @@
             device_id={"tile": other}, device_id_type=MESH,
         )
 
-    images = [
-        remote(measured_hbm.at[:, pl.ds(0, OV)], below, image_send.at[0], image_recv.at[0], up),
-        remote(measured_hbm.at[:, pl.ds(STRIDE - OV, OV)], above, image_send.at[1], image_recv.at[1], down),
-    ]
-    for copy in images:
-        copy.start()
-
-    def edge_copies(number):
-        here = pl.ds(number * GROUP, GROUP)
-        return [
-            remote(edges.at[end, here], near.at[end, here], send_sems.at[end, number], recv_sems.at[end, number], other)
-            for end, other in ((0, up), (1, down))
-        ]
+    sides = ((0, has_above, up), (1, has_below, down))
+    strips = ((pl.ds(0, OV), below), (pl.ds(STRIDE - OV, OV), above))
+
+    def image_copy(end, other):
+        rows, target = strips[end]
+        return remote(measured_hbm.at[:, rows], target, image_send.at[end], image_recv.at[end], other)
+
+    def edge_copy(end, other, number):
+        here = pl.ds(number * width, width)
+        return remote(edges.at[end, here], near.at[end, here], send_sems.at[end, number], recv_sems.at[end, number], other)
+
+    for end, present, other in sides:
+        pl.when(present)(lambda: image_copy(end, other).start())
 
     def wave_copy(number):
-        here = pl.ds(number * GROUP, GROUP)
+        here = pl.ds(number * width, width)
         return pltpu.make_async_copy(waves.at[here], wave_out.at[here], wave_sems.at[number])
 
     def field_of(led):
@@ -180,8 +196,8 @@
         )
 
     def step(number, carry):
-        for inner in range(PAIRS):
-            pair = number * PAIRS + inner
+        for inner in range(FORWARD_PAIRS):
+            pair = number * FORWARD_PAIRS + inner
             field = jnp.concatenate([field_of(2 * pair), field_of(2 * pair + 1)], axis=0)
             mixed = right_product(field, table_ref[0], table_ref[1])
             wave = left_product(table_ref[2], table_ref[3], swap_blocks(mixed))
@@ -196,21 +212,23 @@
                 edges[0, led] = first[:, lo : lo + PUP]
                 edges[1, led] = last[:, lo : lo + PUP]
         wave_copy(number).start()
-        for copy in edge_copies(number):
-            copy.start()
+        for end, present, other in sides:
+            pl.when(present)(lambda: edge_copy(end, other, number).start())
         return carry
 
     lax.fori_loop(0, steps, step, 0)
 
     def finish(number, carry):
         wave_copy(number).wait()
-        for copy in edge_copies(number):
-            copy.wait()
+        for end, present, other in sides:
+            pl.when(present)(lambda: edge_copy(end, other, number).wait_send())
+            pl.when(sides[1 - end][1])(lambda: edge_copy(end, other, number).wait_recv())
         return carry
 
     lax.fori_loop(0, steps, finish, 0)
-    for copy in images:
-        copy.wait()
+    for end, present, other in sides:
+        pl.when(present)(lambda: image_copy(end, other).wait_send())
+        pl.when(sides[1 - end][1])(lambda: image_copy(end, other).wait_recv())
 
 
 def my_place():
@@ -224,8 +242,8 @@
 
 def backward_kernel(
     scale, offsets_hbm, widths_hbm, live_hbm, spec_hbm, pupil_hbm, table_hbm, measured_hbm, above_hbm, below_hbm, edge_hbm, wave_hbm,
-    codes_a_hbm, scales_a_hbm, own_a_hbm, codes_b_hbm, scales_b_hbm, own_b_hbm,
-    spec_out, pupil_out, codes_a, scales_a, own_a, codes_b, scales_b, own_b, waves, planes, offsets_ref, widths_ref, live_ref, order_ref, spec_ref, pupil_ref, table_ref, measured_ref,
+    code_hbm, float_hbm,
+    spec_out, pupil_out, codes, floats, waves, planes, offsets_ref, widths_ref, live_ref, order_ref, spec_ref, pupil_ref, table_ref, measured_ref,
     above_ref, below_ref, edge_ref, sems, wave_sems, out_sems
 ):
     tiles = lax.axis_size("tile")
@@ -274,8 +292,8 @@
     top2 = jnp.concatenate([top, top], axis=1)
     bottom2 = jnp.concatenate([bottom, bottom], axis=1)
     rows = lax.broadcasted_iota(jnp.int32, (OV, 2 * PUP), 0)
-    top_grad = jnp.where((tile > 0) | (rows >= HALF), 2.0 * top2, 0.0)
-    bottom_grad = jnp.where((tile < tiles - 1) | (rows < HALF), 2.0 * bottom2, 0.0)
+    top_inside = (tile > 0) | (rows >= HALF)
+    bottom_inside = (tile < tiles - 1) | (rows < HALF)
     has_above = tile > 0
     has_below = tile < tiles - 1
     lanes = lax.broadcasted_iota(jnp.int32, (PUP, PUP), 1)
@@ -302,10 +320,12 @@
             lower = images(below_ref, leds, 0, HALF)
             near_top = jnp.where(has_above, edges_of(1, leds), 0.0)
             near_bottom = jnp.where(has_below, edges_of(0, leds), 0.0)
-            first = top_grad * (top2 * intensity[:OV] + near_top - jnp.concatenate([upper, own[: OV - HALF]], axis=0))
+            first = 2.0 * top2 * (top2 * intensity[:OV] + near_top - jnp.concatenate([upper, own[: OV - HALF]], axis=0))
             middle = 2.0 * (intensity[OV:STRIDE] - own[HALF : STRIDE - HALF])
-            last = bottom_grad * (bottom2 * intensity[STRIDE:] + near_bottom - jnp.concatenate([own[STRIDE - HALF :], lower], axis=0))
-            grad = alive * jnp.concatenate([first, middle, last], axis=0)
+            last = 2.0 * bottom2 * (bottom2 * intensity[STRIDE:] + near_bottom - jnp.concatenate([own[STRIDE - HALF :], lower], axis=0))
+            grad = alive * jnp.concatenate(
+                [jnp.where(top_inside, first, 0.0), middle, jnp.where(bottom_inside, last, 0.0)], axis=0
+            )
             grad_wave = jnp.concatenate([grad * wave_re, grad * wave_im], axis=0)
             back = right_product(swap_blocks(grad_wave), table_ref[2], table_ref[3])
             grad_field = left_product(table_ref[0], table_ref[1], swap_blocks(back))
@@ -333,52 +353,49 @@
 
     lax.fori_loop(0, steps, step, 0)
     line, place = my_place()
-    depth = SPEC_ROWS
     sends = []
 
     def keep(source, target):
         sends.append(pltpu.make_async_copy(source, target, out_sems.at[len(sends)]))
         sends[-1].start()
 
-    def pieces_of(half, dest):
-        rows = pl.ds(pl.multiple_of(dest * depth, depth), depth)
-        pieces = [spec_out[2 * half + block, part, rows, :] for block in range(2) for part in range(2)]
-        if half == 0:
-            width = PUP_ROWS
-            rows = pl.ds(pl.multiple_of(dest * width, width), width)
+    def pieces_of(chunks, dest):
+        rows = pl.ds(pl.multiple_of(dest * SPEC_ROWS, SPEC_ROWS), SPEC_ROWS)
+        pieces = [spec_out[block, part, rows, :] for block, part in chunks]
+        if chunks is CHUNKS_A:
+            rows = pl.ds(pl.multiple_of(dest * PUP_ROWS, PUP_ROWS), PUP_ROWS)
             pieces += [pupil_out[part, rows, :] for part in range(2)]
         return pieces
 
-    def encode(pieces, codes, scales):
-        start = 0
+    code_rows, float_rows, scale_rows = [0], [0], [OWN_ROWS]
+
+    def encode(pieces):
+        begin = code_rows[0]
         for number, piece in enumerate(pieces):
             most = jnp.maximum(jnp.max(jnp.abs(piece), axis=0, keepdims=True), 1e-30)
-            stop = start + piece.shape[0]
+            start, stop = code_rows[0], code_rows[0] + piece.shape[0]
             codes[start:stop, :] = jnp.round(piece * (LEVELS / most)).astype(jnp.int16)
-            scales[number : number + 1, :] = most * (1.0 / LEVELS)
-            start = stop
-
-    def store(pieces, target):
-        start = 0
+            floats[scale_rows[0] + number : scale_rows[0] + number + 1, :] = most * (1.0 / LEVELS)
+            code_rows[0] = stop
+        scale_rows[0] += 8
+        here = pl.ds(begin, code_rows[0] - begin)
+        keep(codes.at[here], code_hbm.at[here])
+
+    def store(pieces):
         for piece in pieces:
-            stop = start + piece.shape[0]
-            target[start:stop, :] = piece
-            start = stop
-
-    for hop in range(XS):
-        encode(pieces_of(1, dest_of(line + 1, place + 1 + hop)), codes_b.at[hop], scales_b.at[hop])
-        keep(codes_b.at[hop], codes_b_hbm.at[hop])
+            start, stop = float_rows[0], float_rows[0] + piece.shape[0]
+            floats[start:stop, :] = piece
+            float_rows[0] = stop
+
     for turn in range(2):
         for hop in range(XS - 1):
-            encode(pieces_of(0, dest_of(line + 1 + turn, place + 1 + hop)), codes_a.at[turn, hop], scales_a.at[turn, hop])
-            keep(codes_a.at[turn, hop], codes_a_hbm.at[turn, hop])
-        store(pieces_of(0, dest_of(line + 1 + turn, place)), own_a.at[turn])
+            encode(pieces_of(CHUNKS_A, dest_of(line + 1 + turn, place + 1 + hop)))
+        store(pieces_of(CHUNKS_A, dest_of(line + 1 + turn, place)))
     for hop in range(XS):
-        store(pieces_of(1, dest_of(line, place + 1 + hop)), own_b.at[hop])
-    keep(scales_a, scales_a_hbm)
-    keep(scales_b, scales_b_hbm)
-    keep(own_a, own_a_hbm)
-    keep(own_b, own_b_hbm)
+        encode(pieces_of(CHUNKS_B, dest_of(line + 1, place + 1 + hop)))
+    for hop in range(XS):
+        store(pieces_of(CHUNKS_B, dest_of(line, place + 1 + hop)))
+    keep(floats, float_hbm)
     for copy in sends:
         copy.wait()
 
@@ -405,7 +422,7 @@
     rows = shape((lamps, OV, PUP), measured.dtype)
     wave = (lamps, 2 * PUP, PUP)
     edge = (2, lamps, OV, PUP)
-    chunks = lamps // GROUP
+    chunks = lamps // (2 * FORWARD_PAIRS)
     return pl.pallas_call(
         forward_kernel,
         out_shape=(shape(wave, F32), shape(edge, BF16), rows, rows),
@@ -434,30 +451,22 @@
     )(offsets, widths, spectrum, pupil, tables, measured)
 
 
-UNITS = (
-    ((2, XS - 1, ROWS_A, PUP), jnp.int16),
-    ((2, XS - 1, 8, PUP), F32),
-    ((2, ROWS_A, PUP), F32),
-    ((XS, ROWS_B, PUP), jnp.int16),
-    ((XS, 8, PUP), F32),
-    ((XS, ROWS_B, PUP), F32),
-)
-
-
 def backward_call(scale, offsets, widths, live, spectrum, pupil, tables, measured, above, below, edges, waves):
     lamps = measured.shape[0]
     side = spectrum.shape[-1]
     planes = pltpu.VMEM((BLOCKS, 2, side, PUP), F32)
+    slots = -(-lamps // GROUP) * GROUP
     return pl.pallas_call(
         partial(backward_kernel, scale),
-        out_shape=tuple(shape(*unit) for unit in UNITS),
+        out_shape=(shape((CODE_ROWS, PUP), jnp.int16), shape((FLOAT_ROWS, PUP), F32)),
         in_specs=[hbm()] * 11,
-        out_specs=(hbm(),) * 6,
+        out_specs=(hbm(),) * 2,
         scratch_shapes=[
             planes,
             pltpu.VMEM(pupil.shape, F32),
-            *(pltpu.VMEM(*unit) for unit in UNITS),
-            pltpu.VMEM(waves.shape, F32),
+            pltpu.VMEM((CODE_ROWS, PUP), jnp.int16),
+            pltpu.VMEM((FLOAT_ROWS, PUP), F32),
+            pltpu.VMEM((slots, 2 * PUP, PUP), F32),
             planes,
             pltpu.SMEM(offsets.shape, jnp.int32),
             pltpu.SMEM(widths.shape, jnp.int32),
@@ -471,8 +480,8 @@
             pltpu.VMEM(below.shape, below.dtype),
             pltpu.VMEM(edges.shape, edges.dtype),
             pltpu.SemaphoreType.DMA((10,)),
-            pltpu.SemaphoreType.DMA((lamps,)),
-            pltpu.SemaphoreType.DMA((14,)),
+            pltpu.SemaphoreType.DMA((slots,)),
+            pltpu.SemaphoreType.DMA((SENT_A + SENT_B + 1,)),
         ],
         compiler_params=pltpu.CompilerParams(vmem_limit_bytes=VMEM_LIMIT),
         name="backward",
@@ -480,17 +489,11 @@
 
 
 def gather_kernel(
-    codes_a, scales_a, own_a_hbm, codes_b, scales_b, own_b_hbm, spec_out, pupil_out,
-    own_a, own_b, held_a, held_scales_a, held_b, held_scales_b, code_a2, scale_a2, held_a2, held_scales_a2,
-    codes_b2, scales_b2, held_b2, held_scales_b2, local_sems, send_sems, recv_sems
+    code_hbm, float_hbm, spec_out, pupil_out, own, held, held_scales, codes2, scales2, held2, held_scales2, own_sem, send_sems, recv_sems
 ):
     line, place = my_place()
-    local = [
-        pltpu.make_async_copy(own_a_hbm, own_a, local_sems.at[0]),
-        pltpu.make_async_copy(own_b_hbm, own_b, local_sems.at[1]),
-    ]
-    for copy in local:
-        copy.start()
+    own_copy = pltpu.make_async_copy(float_hbm.at[pl.ds(0, OWN_ROWS)], own, own_sem)
+    own_copy.start()
     opposite = dest_of(line + 1, place)
     beside = [dest_of(line, place + 1 + hop) for hop in range(XS - 1)]
     barrier = pltpu.get_barrier_semaphore()
@@ -499,9 +502,9 @@
     pl.semaphore_wait(barrier, XS)
     used = [0]
 
-    def send(source, target, scale_source, scale_target, other):
+    def send(codes, scales, targets, other):
         pair = []
-        for src, dst in ((source, target), (scale_source, scale_target)):
+        for src, dst in zip((codes, scales), targets):
             number = used[0]
             used[0] += 1
             pair.append(
@@ -511,107 +514,89 @@
                 )
             )
             pair[-1].start()
-        return pair
-
-    first_a = [[None] * (XS - 1), [None] * (XS - 1)]
-    first_b = [None] * XS
-    for hop in range(XS):
-        first_b[hop] = send(codes_b.at[hop], held_b.at[hop], scales_b.at[hop], held_scales_b.at[hop], opposite)
-        if hop < XS - 1:
-            first_a[0][hop] = send(
-                codes_a.at[0, hop], held_a.at[0, hop], scales_a.at[0, hop], held_scales_a.at[0, hop], beside[hop]
-            )
-    for hop in range(XS - 1):
-        first_a[1][hop] = send(
-            codes_a.at[1, hop], held_a.at[1, hop], scales_a.at[1, hop], held_scales_a.at[1, hop], beside[hop]
-        )
-    for copy in local:
-        copy.wait()
-
-    def arrived(pair):
-        for copy in pair:
+        return pair, targets
+
+    def arrive(message):
+        for copy in message[0]:
             copy.wait()
-
-    bounds_b = [(number * SPEC_ROWS, (number + 1) * SPEC_ROWS) for number in range(4)]
-    bounds_a = bounds_b + [(ROWS_B + part * PUP_ROWS, ROWS_B + (part + 1) * PUP_ROWS) for part in range(2)]
-
-    def total(own, parts, number, start, stop):
-        value = own[start:stop, :]
+        return message[1]
+
+    def first(number, other):
+        rows = ROWS_A if number < SENT_A else ROWS_B
+        start = number * ROWS_A if number < SENT_A else SENT_A * ROWS_A + (number - SENT_A) * ROWS_B
+        here, scale = pl.ds(start, rows), pl.ds(8 * number, 8)
+        source_scale = pl.ds(OWN_ROWS + 8 * number, 8)
+        return send(code_hbm.at[here], float_hbm.at[source_scale], (held.at[here], held_scales.at[scale]), other)
+
+    def second(number, other):
+        here, scale = second_rows(number), pl.ds(8 * number, 8)
+        return send(codes2.at[here], scales2.at[scale], (held2.at[here], held_scales2.at[scale]), other)
+
+    def second_rows(number):
+        return pl.ds(0, ROWS_A) if number == 0 else pl.ds(ROWS_A + (number - 1) * ROWS_B, ROWS_B)
+
+    def total(start, parts, number, bounds):
+        value = own[start + bounds[0] : start + bounds[1], :]
         for codes, scales in parts:
-            value += codes[start:stop, :].astype(F32) * scales[number : number + 1, :]
+            value += codes[bounds[0] : bounds[1], :].astype(F32) * scales[number : number + 1, :]
         return value
 
-    def encode(own, parts, bounds, codes, scales):
-        for number, (start, stop) in enumerate(bounds):
-            value = total(own, parts, number, start, stop)
+    def encode(start, parts, bounds, number):
+        codes, scales = codes2.at[second_rows(number)], scales2.at[pl.ds(8 * number, 8)]
+        for index, (low, high) in enumerate(bounds):
+            value = total(start, parts, index, (low, high))
             most = jnp.maximum(jnp.max(jnp.abs(value), axis=0, keepdims=True), 1e-30)
-            codes[start:stop, :] = jnp.round(value * (LEVELS / most)).astype(jnp.int16)
-            scales[number : number + 1, :] = most * (1.0 / LEVELS)
-
-    second_b = [None] * (XS - 1)
-
-    def pass_on(hop):
-        arrived(first_b[hop])
-        parts = [(held_b.at[hop], held_scales_b.at[hop])]
-        encode(own_b.at[hop], parts, bounds_b, codes_b2.at[hop], scales_b2.at[hop])
-        second_b[hop] = send(codes_b2.at[hop], held_b2.at[hop], scales_b2.at[hop], held_scales_b2.at[hop], beside[hop])
-
-    pass_on(0)
-    pass_on(1)
-    for hop in range(XS - 1):
-        arrived(first_a[0][hop])
-    parts = [(held_a.at[0, hop], held_scales_a.at[0, hop]) for hop in range(XS - 1)]
-    encode(own_a.at[0], parts, bounds_a, code_a2, scale_a2)
-    second_a = send(code_a2, held_a2, scale_a2, held_scales_a2, opposite)
-    pass_on(2)
-    for hop in range(XS - 1):
-        arrived(first_a[1][hop])
-    arrived(second_a)
-    parts = [(held_a.at[1, hop], held_scales_a.at[1, hop]) for hop in range(XS - 1)] + [(held_a2, held_scales_a2)]
-    for number, (start, stop) in enumerate(bounds_a):
-        value = total(own_a.at[1], parts, number, start, stop)
-        if number < 4:
-            block, part = number // 2, number % 2
+            codes[low:high, :] = jnp.round(value * (LEVELS / most)).astype(jnp.int16)
+            scales[index : index + 1, :] = most * (1.0 / LEVELS)
+
+    hops = range(XS - 1)
+    start_b = 2 * ROWS_A
+    first_b, first_a, last_a, second_b = [], [], [], []
+    for hop in hops:
+        first_b.append(first(SENT_A + hop, opposite))
+        first_a.append(first(hop, beside[hop]))
+    first_b.append(first(SENT_A + XS - 1, opposite))
+    own_copy.wait()
+    for hop in hops:
+        if hop == XS - 2:
+            encode(0, [arrive(message) for message in first_a], BOUNDS_A, 0)
+            second_a = second(0, opposite)
+        encode(start_b + hop * ROWS_B, [arrive(first_b[hop])], BOUNDS_B, 1 + hop)
+        second_b.append(second(1 + hop, beside[hop]))
+        last_a.append(first(XS - 1 + hop, beside[hop]))
+
+    def put(chunks, number, value):
+        if number < len(chunks):
+            block, part = chunks[number]
             spec_out[part, :, block * PUP : (block + 1) * PUP] = value
         else:
-            pupil_out[number - 4] = value
-    arrived(first_b[XS - 1])
-    for hop in range(XS - 1):
-        arrived(second_b[hop])
-    parts = [(held_b.at[XS - 1], held_scales_b.at[XS - 1])]
-    parts += [(held_b2.at[hop], held_scales_b2.at[hop]) for hop in range(XS - 1)]
-    for number, (start, stop) in enumerate(bounds_b):
-        block, part = 2 + number // 2, number % 2
-        spec_out[part, :, block * PUP : (block + 1) * PUP] = total(own_b.at[XS - 1], parts, number, start, stop)
-
-
-def gather_call(codes_a, scales_a, own_a, codes_b, scales_b, own_b):
-    moved = 2 * (2 * (XS - 1) + XS + 1 + XS - 1)
-    code2 = pltpu.VMEM((ROWS_A, PUP), jnp.int16)
-    scale2 = pltpu.VMEM((8, PUP), F32)
-    codes2 = pltpu.VMEM((XS - 1, ROWS_B, PUP), jnp.int16)
-    scales2 = pltpu.VMEM((XS - 1, 8, PUP), F32)
+            pupil_out[number - len(chunks)] = value
+
+    parts = [arrive(first_b[XS - 1]), *(arrive(message) for message in second_b)]
+    for number, bounds in enumerate(BOUNDS_B):
+        put(CHUNKS_B, number, total(start_b + (XS - 1) * ROWS_B, parts, number, bounds))
+    parts = [*(arrive(message) for message in last_a), arrive(second_a)]
+    for number, bounds in enumerate(BOUNDS_A):
+        put(CHUNKS_A, number, total(ROWS_A, parts, number, bounds))
+
+
+def gather_call(codes, floats):
+    moved = 2 * (SENT_A + SENT_B + XS)
+    second = (ROWS_A + (XS - 1) * ROWS_B, PUP)
     return pl.pallas_call(
         gather_kernel,
         out_shape=(shape((2, SPEC_ROWS, BLOCKS * PUP), F32), shape((2, PUP_ROWS, PUP), F32)),
-        in_specs=[hbm()] * 6,
+        in_specs=[hbm()] * 2,
         out_specs=(vmem(), vmem()),
         scratch_shapes=[
-            pltpu.VMEM(own_a.shape, F32),
-            pltpu.VMEM(own_b.shape, F32),
-            pltpu.VMEM(codes_a.shape, codes_a.dtype),
-            pltpu.VMEM(scales_a.shape, F32),
-            pltpu.VMEM(codes_b.shape, codes_b.dtype),
-            pltpu.VMEM(scales_b.shape, F32),
-            code2,
-            scale2,
-            code2,
-            scale2,
-            codes2,
-            scales2,
-            codes2,
-            scales2,
-            pltpu.SemaphoreType.DMA((2,)),
+            pltpu.VMEM((OWN_ROWS, PUP), F32),
+            pltpu.VMEM((CODE_ROWS, PUP), jnp.int16),
+            pltpu.VMEM((8 * (SENT_A + SENT_B), PUP), F32),
+            pltpu.VMEM(second, jnp.int16),
+            pltpu.VMEM((8 * XS, PUP), F32),
+            pltpu.VMEM(second, jnp.int16),
+            pltpu.VMEM((8 * XS, PUP), F32),
+            pltpu.SemaphoreType.DMA,
             pltpu.SemaphoreType.DMA((moved,)),
             pltpu.SemaphoreType.DMA((moved,)),
         ],
@@ -619,7 +604,7 @@
             collective_id=2, has_side_effects=True, vmem_limit_bytes=GATHER_LIMIT
         ),
         name="reduce_scatter",
-    )(codes_a, scales_a, own_a, codes_b, scales_b, own_b)
+    )(codes, floats)
 
 
 def on_device(tables, spectrum, pupil, offsets, widths, live, measured):

time: 50.8 us -> 41.6 us (0.82)
  the two profiles are of different devices: /device:TPU:2 before, /device:TPU:1 now
where the time goes in v3:
time: 41.6 us; the launch traced here: 41.4 us
  Pallas kernels  39.4 us (95%)
  local copies, waits for them, and re-layouts  1.31 us (3%)
  between operations  0.65 us (2%)
    pallas_call x1, Pallas kernels, gather_call(): pl.pallas_call(gather_kernel, out_shape=(shape((2, SPEC_ROWS, BLOCKS * PU...  15.9 us
    pallas_call x1, Pallas kernels, forward_call(): pl.pallas_call(forward_kernel, out_shape=(shape(wave, F32), shape(edge, B...  14.1 us
    pallas_call x1, Pallas kernels, backward_call(): pl.pallas_call(partial(backward_kernel, scale), out_shape=(shape((CODE_RO...  9.42 us
    unnamed x2, local copies, waits for them, and re-layouts  1.31 us

profile of v3, /device:TPU:1, one launch (start us, length us, event | category | flops | bytes accessed | tf_op | source)
XLA Modules:
  0.0 41.4 jit_solution(12131886819797173280)
XLA Ops:
  0.6 14.1 %forward.1 = (f32[28,256,128]{2,1,0:T(8,128)}, bf16[2,28,16,128]{3,2,1,0:T(8,128)(2,1)}, bf16[28,16,128]{2,1,0:T(8,128)(2,1)}, bf16[28,16,128]{2,1,0:T(8,128)(2,1)}) custom-call(s32[2,28]{1,0:T(2,128)} %bitcast.13, s32[63]{0:T(128)} %widths_hbm.3, bf16[2,512,512]{2,1,0:T(8,128)(2,1)} %bitcast.9, bf16[2,128,128]{2,1,0:T(8,128)(2,1)} %bitcast.11, ...), custom_call_target="tpu_custom_call" | custom-call | tf_op jit(solution)/shard_map/forward/pallas_call | solution.py:426
  14.7 9.4 %backward.1 = (s16[2624,128]{1,0:T(8,128)(2,1)}, f32[1808,128]{1,0:T(8,128)}) custom-call(s32[2,28]{1,0:T(2,128)} %bitcast.14, s32[63]{0:T(128)} %widths_hbm.3, s32[28]{0:T(128)} %live_hbm.1, bf16[2,512,512]{2,1,0:T(8,128)(2,1)} %bitcast.10, bf16[2,128,128]{2,1,0:T(8,128)(2,1)} %bitcast.12, bf16[4,256,256]{2,1,0:T(8,128)(2,1)} %constant.2.clone.table_hbm, ...), custom_call_target="tpu_custom_call" | custom-call | tf_op jit(solution)/shard_map/backward/pallas_call | solution.py:459
  24.1 15.9 %reduce_scatter.1 = (f32[2,64,512]{2,1,0:T(8,128)S(1)}, f32[2,16,128]{2,1,0:T(8,128)S(1)}) custom-call(s16[2624,128]{1,0:T(8,128)(2,1)} %get-tuple-element.14.code_hbm, f32[1808,128]{1,0:T(8,128)} %get-tuple-element.15.float_hbm), custom_call_target="tpu_custom_call" | custom-call | tf_op jit(solution)/shard_map/reduce_scatter/pallas_call | solution.py:586
  40.1 0.7 %copy.11 = f32[1,2,64,512]{3,2,1,0:T(8,128)} copy(f32[1,2,64,512]{3,2,1,0:T(8,128)S(1)} %bitcast.7) | data formatting | bytes 524288
  40.8 0.6 %copy.12 = f32[1,2,16,128]{3,2,1,0:T(8,128)} copy(f32[1,2,16,128]{3,2,1,0:T(8,128)S(1)} %bitcast.8) | data formatting | bytes 32768

commit v4 on v3

--- a/solution.py
+++ b/solution.py
@@ -36,8 +36,7 @@
 FORWARD_PAIRS = 7
 PAIRS = 4
 GROUP = 2 * PAIRS
-VMEM_LIMIT = 63 * 1024 * 1024
-GATHER_LIMIT = 213 * 256 * 1024
+VMEM_LIMIT = 24 * 1024 * 1024
 
 
 def dft_tables():
@@ -120,9 +119,8 @@
 
 def forward_kernel(
     offsets_hbm, widths_hbm, spec_hbm, pupil_hbm, table_hbm, measured_hbm,
-    wave_out, near, above, below,
-    waves, edges, planes, offsets_ref, widths_ref, spec_ref, pupil_ref, table_ref,
-    local_sems, wave_sems, send_sems, recv_sems, image_send, image_recv
+    waves, near, above, below, planes, pupil_ref, table_ref, measured_ref,
+    edges, offsets_ref, widths_ref, spec_ref, local_sems, send_sems, recv_sems, image_send, image_recv
 ):
     tiles = lax.axis_size("tile")
     tile = lax.axis_index("tile")
@@ -138,6 +136,7 @@
                 (spec_hbm, spec_ref),
                 (pupil_hbm, pupil_ref),
                 (table_hbm, table_ref),
+                (measured_hbm, measured_ref),
             )
         )
     ]
@@ -157,7 +156,7 @@
     top, bottom = ramp_weights(widths_ref, tile, tiles)
     top2 = jnp.concatenate([top, top], axis=1)
     bottom2 = jnp.concatenate([bottom, bottom], axis=1)
-    for copy in local[3:]:
+    for copy in local[3:5]:
         copy.wait()
     pl.semaphore_wait(barrier, has_above.astype(jnp.int32) + has_below.astype(jnp.int32))
 
@@ -180,10 +179,6 @@
 
     for end, present, other in sides:
         pl.when(present)(lambda: image_copy(end, other).start())
-
-    def wave_copy(number):
-        here = pl.ds(number * width, width)
-        return pltpu.make_async_copy(waves.at[here], wave_out.at[here], wave_sems.at[number])
 
     def field_of(led):
         row, col = offsets_ref[0, led], offsets_ref[1, led]
@@ -211,7 +206,6 @@
                 waves[led] = wave[:, lo : lo + PUP]
                 edges[0, led] = first[:, lo : lo + PUP]
                 edges[1, led] = last[:, lo : lo + PUP]
-        wave_copy(number).start()
         for end, present, other in sides:
             pl.when(present)(lambda: edge_copy(end, other, number).start())
         return carry
@@ -219,13 +213,13 @@
     lax.fori_loop(0, steps, step, 0)
 
     def finish(number, carry):
-        wave_copy(number).wait()
         for end, present, other in sides:
             pl.when(present)(lambda: edge_copy(end, other, number).wait_send())
             pl.when(sides[1 - end][1])(lambda: edge_copy(end, other, number).wait_recv())
         return carry
 
     lax.fori_loop(0, steps, finish, 0)
+    local[5].wait()
     for end, present, other in sides:
         pl.when(present)(lambda: image_copy(end, other).wait_send())
         pl.when(sides[1 - end][1])(lambda: image_copy(end, other).wait_recv())
@@ -241,53 +235,26 @@
 
 
 def backward_kernel(
-    scale, offsets_hbm, widths_hbm, live_hbm, spec_hbm, pupil_hbm, table_hbm, measured_hbm, above_hbm, below_hbm, edge_hbm, wave_hbm,
-    code_hbm, float_hbm,
-    spec_out, pupil_out, codes, floats, waves, planes, offsets_ref, widths_ref, live_ref, order_ref, spec_ref, pupil_ref, table_ref, measured_ref,
-    above_ref, below_ref, edge_ref, sems, wave_sems, out_sems
+    scale, offsets_hbm, widths_hbm, live_hbm, planes, pupil_ref, table_ref, measured_ref, above_ref, below_ref, edge_ref, waves,
+    codes, floats, spec_out, pupil_out, offsets_ref, widths_ref, live_ref, order_ref, sems
 ):
     tiles = lax.axis_size("tile")
     tile = lax.axis_index("tile")
     local = [
         pltpu.make_async_copy(source, target, sems.at[number])
         for number, (source, target) in enumerate(
-            (
-                (offsets_hbm, offsets_ref),
-                (widths_hbm, widths_ref),
-                (live_hbm, live_ref),
-                (spec_hbm, spec_ref),
-                (pupil_hbm, pupil_ref),
-                (table_hbm, table_ref),
-                (measured_hbm, measured_ref),
-                (above_hbm, above_ref),
-                (below_hbm, below_ref),
-                (edge_hbm, edge_ref),
-            )
+            ((offsets_hbm, offsets_ref), (widths_hbm, widths_ref), (live_hbm, live_ref))
         )
     ]
     for copy in local:
         copy.start()
-
-    for copy in local[:3]:
+    spec_out[...] = jnp.zeros_like(spec_out)
+    pupil_out[...] = jnp.zeros_like(pupil_out)
+    for copy in local:
         copy.wait()
     count = list_live(live_ref, order_ref)
     steps = (count + GROUP - 1) // GROUP
 
-    def wave_copy(slot):
-        return pltpu.make_async_copy(wave_hbm.at[order_ref[slot]], waves.at[slot], wave_sems.at[slot])
-
-    def fetch(slot, carry):
-        wave_copy(slot).start()
-        return carry
-
-    lax.fori_loop(0, steps * GROUP, fetch, 0)
-
-    spec_out[...] = jnp.zeros_like(spec_out)
-    pupil_out[...] = jnp.zeros_like(pupil_out)
-    local[3].wait()
-    load_spectrum(spec_ref, planes)
-    for copy in local[4:]:
-        copy.wait()
     top, bottom = ramp_weights(widths_ref, tile, tiles)
     top2 = jnp.concatenate([top, top], axis=1)
     bottom2 = jnp.concatenate([bottom, bottom], axis=1)
@@ -305,14 +272,12 @@
         return jnp.concatenate([ref[led, low:high].astype(F32) for led in leds], axis=1)
 
     def step(number, carry):
-        for inner in range(GROUP):
-            wave_copy(number * GROUP + inner).wait()
         for inner in range(PAIRS):
             pair = number * PAIRS + inner
             leds = order_ref[2 * pair], order_ref[2 * pair + 1]
             side_of = lax.broadcasted_iota(jnp.int32, (1, 2 * PUP), 1) // PUP
             alive = jnp.where(2 * pair + side_of < count, scale, 0.0)
-            wave = jnp.concatenate([waves[2 * pair], waves[2 * pair + 1]], axis=1)
+            wave = jnp.concatenate([waves[led] for led in leds], axis=1)
             wave_re, wave_im = wave[:PUP], wave[PUP:]
             intensity = wave_re * wave_re + wave_im * wave_im
             own = images(measured_ref, leds, 0, STRIDE)
@@ -353,11 +318,6 @@
 
     lax.fori_loop(0, steps, step, 0)
     line, place = my_place()
-    sends = []
-
-    def keep(source, target):
-        sends.append(pltpu.make_async_copy(source, target, out_sems.at[len(sends)]))
-        sends[-1].start()
 
     def pieces_of(chunks, dest):
         rows = pl.ds(pl.multiple_of(dest * SPEC_ROWS, SPEC_ROWS), SPEC_ROWS)
@@ -370,7 +330,6 @@
     code_rows, float_rows, scale_rows = [0], [0], [OWN_ROWS]
 
     def encode(pieces):
-        begin = code_rows[0]
         for number, piece in enumerate(pieces):
             most = jnp.maximum(jnp.max(jnp.abs(piece), axis=0, keepdims=True), 1e-30)
             start, stop = code_rows[0], code_rows[0] + piece.shape[0]
@@ -378,8 +337,6 @@
             floats[scale_rows[0] + number : scale_rows[0] + number + 1, :] = most * (1.0 / LEVELS)
             code_rows[0] = stop
         scale_rows[0] += 8
-        here = pl.ds(begin, code_rows[0] - begin)
-        keep(codes.at[here], code_hbm.at[here])
 
     def store(pieces):
         for piece in pieces:
@@ -395,50 +352,50 @@
         encode(pieces_of(CHUNKS_B, dest_of(line + 1, place + 1 + hop)))
     for hop in range(XS):
         store(pieces_of(CHUNKS_B, dest_of(line, place + 1 + hop)))
-    keep(floats, float_hbm)
-    for copy in sends:
-        copy.wait()
 
 
 def vmem():
     return pl.BlockSpec(memory_space=pltpu.VMEM)
 
 
-def smem():
-    return pl.BlockSpec(memory_space=pltpu.SMEM)
-
-
 def hbm():
     return pl.BlockSpec(memory_space=pltpu.HBM)
 
 
-def shape(dims, dtype):
-    return jax.ShapeDtypeStruct(dims, dtype)
+def in_hbm(*arrays):
+    return [pltpu.with_memory_space_constraint(array, pltpu.HBM) for array in arrays]
+
+
+def in_vmem(*arrays):
+    return [pltpu.with_memory_space_constraint(array, pltpu.VMEM) for array in arrays]
 
 
 def forward_call(offsets, widths, spectrum, pupil, tables, measured):
     lamps = measured.shape[0]
     side = spectrum.shape[-1]
-    rows = shape((lamps, OV, PUP), measured.dtype)
-    wave = (lamps, 2 * PUP, PUP)
-    edge = (2, lamps, OV, PUP)
+    rows = pltpu.VMEM((lamps, OV, PUP), measured.dtype)
+    edge = pltpu.VMEM((2, lamps, OV, PUP), BF16)
     chunks = lamps // (2 * FORWARD_PAIRS)
     return pl.pallas_call(
         forward_kernel,
-        out_shape=(shape(wave, F32), shape(edge, BF16), rows, rows),
+        out_shape=(
+            pltpu.VMEM((lamps, 2 * PUP, PUP), F32),
+            edge,
+            rows,
+            rows,
+            pltpu.VMEM((BLOCKS, 2, side, PUP), F32),
+            pltpu.VMEM(pupil.shape, pupil.dtype),
+            pltpu.VMEM(tables.shape, tables.dtype),
+            pltpu.VMEM(measured.shape, measured.dtype),
+        ),
         in_specs=[hbm()] * 6,
-        out_specs=(hbm(),) * 4,
+        out_specs=(vmem(),) * 8,
         scratch_shapes=[
-            pltpu.VMEM(wave, F32),
-            pltpu.VMEM(edge, BF16),
-            pltpu.VMEM((BLOCKS, 2, side, PUP), F32),
+            edge,
             pltpu.SMEM(offsets.shape, jnp.int32),
             pltpu.SMEM(widths.shape, jnp.int32),
             pltpu.VMEM(spectrum.shape, spectrum.dtype),
-            pltpu.VMEM(pupil.shape, pupil.dtype),
-            pltpu.VMEM(tables.shape, tables.dtype),
-            pltpu.SemaphoreType.DMA((5,)),
-            pltpu.SemaphoreType.DMA((chunks,)),
+            pltpu.SemaphoreType.DMA((6,)),
             pltpu.SemaphoreType.DMA((2, chunks)),
             pltpu.SemaphoreType.DMA((2, chunks)),
             pltpu.SemaphoreType.DMA((2,)),
@@ -448,52 +405,34 @@
             collective_id=1, has_side_effects=True, vmem_limit_bytes=VMEM_LIMIT
         ),
         name="forward",
-    )(offsets, widths, spectrum, pupil, tables, measured)
-
-
-def backward_call(scale, offsets, widths, live, spectrum, pupil, tables, measured, above, below, edges, waves):
+    )(*in_hbm(offsets, widths, spectrum, pupil, tables, measured))
+
+
+def backward_call(scale, offsets, widths, live, planes, pupil, tables, measured, above, below, edges, waves):
     lamps = measured.shape[0]
-    side = spectrum.shape[-1]
-    planes = pltpu.VMEM((BLOCKS, 2, side, PUP), F32)
-    slots = -(-lamps // GROUP) * GROUP
     return pl.pallas_call(
         partial(backward_kernel, scale),
-        out_shape=(shape((CODE_ROWS, PUP), jnp.int16), shape((FLOAT_ROWS, PUP), F32)),
-        in_specs=[hbm()] * 11,
-        out_specs=(hbm(),) * 2,
+        out_shape=(pltpu.VMEM((CODE_ROWS, PUP), jnp.int16), pltpu.VMEM((FLOAT_ROWS, PUP), F32)),
+        in_specs=[hbm()] * 3 + [vmem()] * 8,
+        out_specs=(vmem(), vmem()),
         scratch_shapes=[
-            planes,
+            pltpu.VMEM(planes.shape, F32),
             pltpu.VMEM(pupil.shape, F32),
-            pltpu.VMEM((CODE_ROWS, PUP), jnp.int16),
-            pltpu.VMEM((FLOAT_ROWS, PUP), F32),
-            pltpu.VMEM((slots, 2 * PUP, PUP), F32),
-            planes,
             pltpu.SMEM(offsets.shape, jnp.int32),
             pltpu.SMEM(widths.shape, jnp.int32),
             pltpu.SMEM(live.shape, jnp.int32),
             pltpu.SMEM((lamps + GROUP,), jnp.int32),
-            pltpu.VMEM(spectrum.shape, spectrum.dtype),
-            pltpu.VMEM(pupil.shape, pupil.dtype),
-            pltpu.VMEM(tables.shape, tables.dtype),
-            pltpu.VMEM(measured.shape, measured.dtype),
-            pltpu.VMEM(above.shape, above.dtype),
-            pltpu.VMEM(below.shape, below.dtype),
-            pltpu.VMEM(edges.shape, edges.dtype),
-            pltpu.SemaphoreType.DMA((10,)),
-            pltpu.SemaphoreType.DMA((slots,)),
-            pltpu.SemaphoreType.DMA((SENT_A + SENT_B + 1,)),
+            pltpu.SemaphoreType.DMA((3,)),
         ],
         compiler_params=pltpu.CompilerParams(vmem_limit_bytes=VMEM_LIMIT),
         name="backward",
-    )(offsets, widths, live, spectrum, pupil, tables, measured, above, below, edges, waves)
+    )(*in_hbm(offsets, widths, live), *in_vmem(planes, pupil, tables, measured, above, below, edges, waves))
 
 
 def gather_kernel(
-    code_hbm, float_hbm, spec_out, pupil_out, own, held, held_scales, codes2, scales2, held2, held_scales2, own_sem, send_sems, recv_sems
+    codes, floats, spec_out, pupil_out, held, held_scales, codes2, scales2, held2, held_scales2, send_sems, recv_sems
 ):
     line, place = my_place()
-    own_copy = pltpu.make_async_copy(float_hbm.at[pl.ds(0, OWN_ROWS)], own, own_sem)
-    own_copy.start()
     opposite = dest_of(line + 1, place)
     beside = [dest_of(line, place + 1 + hop) for hop in range(XS - 1)]
     barrier = pltpu.get_barrier_semaphore()
@@ -502,9 +441,9 @@
     pl.semaphore_wait(barrier, XS)
     used = [0]
 
-    def send(codes, scales, targets, other):
+    def send(code, scale, targets, other):
         pair = []
-        for src, dst in zip((codes, scales), targets):
+        for src, dst in zip((code, scale), targets):
             number = used[0]
             used[0] += 1
             pair.append(
@@ -526,7 +465,7 @@
         start = number * ROWS_A if number < SENT_A else SENT_A * ROWS_A + (number - SENT_A) * ROWS_B
         here, scale = pl.ds(start, rows), pl.ds(8 * number, 8)
         source_scale = pl.ds(OWN_ROWS + 8 * number, 8)
-        return send(code_hbm.at[here], float_hbm.at[source_scale], (held.at[here], held_scales.at[scale]), other)
+        return send(codes.at[here], floats.at[source_scale], (held.at[here], held_scales.at[scale]), other)
 
     def second(number, other):
         here, scale = second_rows(number), pl.ds(8 * number, 8)
@@ -536,18 +475,18 @@
         return pl.ds(0, ROWS_A) if number == 0 else pl.ds(ROWS_A + (number - 1) * ROWS_B, ROWS_B)
 
     def total(start, parts, number, bounds):
-        value = own[start + bounds[0] : start + bounds[1], :]
-        for codes, scales in parts:
-            value += codes[bounds[0] : bounds[1], :].astype(F32) * scales[number : number + 1, :]
+        value = floats[start + bounds[0] : start + bounds[1], :]
+        for code, scale in parts:
+            value += code[bounds[0] : bounds[1], :].astype(F32) * scale[number : number + 1, :]
         return value
 
     def encode(start, parts, bounds, number):
-        codes, scales = codes2.at[second_rows(number)], scales2.at[pl.ds(8 * number, 8)]
+        code, scale = codes2.at[second_rows(number)], scales2.at[pl.ds(8 * number, 8)]
         for index, (low, high) in enumerate(bounds):
             value = total(start, parts, index, (low, high))
             most = jnp.maximum(jnp.max(jnp.abs(value), axis=0, keepdims=True), 1e-30)
-            codes[low:high, :] = jnp.round(value * (LEVELS / most)).astype(jnp.int16)
-            scales[index : index + 1, :] = most * (1.0 / LEVELS)
+            code[low:high, :] = jnp.round(value * (LEVELS / most)).astype(jnp.int16)
+            scale[index : index + 1, :] = most * (1.0 / LEVELS)
 
     hops = range(XS - 1)
     start_b = 2 * ROWS_A
@@ -556,7 +495,6 @@
         first_b.append(first(SENT_A + hop, opposite))
         first_a.append(first(hop, beside[hop]))
     first_b.append(first(SENT_A + XS - 1, opposite))
-    own_copy.wait()
     for hop in hops:
         if hop == XS - 2:
             encode(0, [arrive(message) for message in first_a], BOUNDS_A, 0)
@@ -585,26 +523,27 @@
     second = (ROWS_A + (XS - 1) * ROWS_B, PUP)
     return pl.pallas_call(
         gather_kernel,
-        out_shape=(shape((2, SPEC_ROWS, BLOCKS * PUP), F32), shape((2, PUP_ROWS, PUP), F32)),
-        in_specs=[hbm()] * 2,
+        out_shape=(
+            pltpu.VMEM((2, SPEC_ROWS, BLOCKS * PUP), F32),
+            pltpu.VMEM((2, PUP_ROWS, PUP), F32),
+        ),
+        in_specs=[vmem()] * 2,
         out_specs=(vmem(), vmem()),
         scratch_shapes=[
-            pltpu.VMEM((OWN_ROWS, PUP), F32),
             pltpu.VMEM((CODE_ROWS, PUP), jnp.int16),
             pltpu.VMEM((8 * (SENT_A + SENT_B), PUP), F32),
             pltpu.VMEM(second, jnp.int16),
             pltpu.VMEM((8 * XS, PUP), F32),
             pltpu.VMEM(second, jnp.int16),
             pltpu.VMEM((8 * XS, PUP), F32),
-            pltpu.SemaphoreType.DMA,
             pltpu.SemaphoreType.DMA((moved,)),
             pltpu.SemaphoreType.DMA((moved,)),
         ],
         compiler_params=pltpu.CompilerParams(
-            collective_id=2, has_side_effects=True, vmem_limit_bytes=GATHER_LIMIT
+            collective_id=2, has_side_effects=True, vmem_limit_bytes=VMEM_LIMIT
         ),
         name="reduce_scatter",
-    )(codes, floats)
+    )(*in_vmem(codes, floats))
 
 
 def on_device(tables, spectrum, pupil, offsets, widths, live, measured):
@@ -612,9 +551,11 @@
     lamps = measured.shape[0]
     scale = 1.0 / math.sqrt(lamps * groups)
     spectrum, pupil, offsets = spectrum[0], pupil[0], offsets[0].T
-    waves, near, above, below = forward_call(offsets, widths, spectrum, pupil, tables, measured)
+    waves, near, above, below, planes, pupil, tables, measured = forward_call(
+        offsets, widths, spectrum, pupil, tables, measured
+    )
     parts = backward_call(
-        scale, offsets, widths, live, spectrum, pupil, tables, measured, above, below, near, waves
+        scale, offsets, widths, live, planes, pupil, tables, measured, above, below, near, waves
     )
     spec_share, pupil_share = gather_call(*parts)
     return spec_share[None], pupil_share[None]

time: 41.6 us -> 38.1 us (0.916)
  Pallas kernels: 39.4 us -> 35.7 us
    pallas_call x3, Pallas kernels: 39.4 us -> 35.7 us  [the longest x1 15.4 us: gather_call(): pl.pallas_call(gather_kernel, out_shape=(pltpu.VMEM((2, SPEC_ROWS, BLOCKS...]
where the time goes in v4:
time: 38.1 us; the launch traced here: 37.7 us
  Pallas kernels  35.7 us (94%)
  local copies, waits for them, and re-layouts  1.31 us (3%)
  between operations  0.65 us (2%)
    pallas_call x1, Pallas kernels, gather_call(): pl.pallas_call(gather_kernel, out_shape=(pltpu.VMEM((2, SPEC_ROWS, BLOCKS...  15.4 us
    pallas_call x1, Pallas kernels, forward_call(): pl.pallas_call(forward_kernel, out_shape=(pltpu.VMEM((lamps, 2 * PUP, PUP...  13.9 us
    pallas_call x1, Pallas kernels, backward_call(): pl.pallas_call(partial(backward_kernel, scale), out_shape=(pltpu.VMEM((CO...  6.4 us
    unnamed x2, local copies, waits for them, and re-layouts  1.31 us

profile of v4, /device:TPU:1, one launch (start us, length us, event | category | flops | bytes accessed | tf_op | source)
XLA Modules:
  0.0 37.7 jit_solution(7403950070654177370)
XLA Ops:
  0.6 13.9 %forward.1 = (f32[28,256,128]{2,1,0:T(8,128)S(1)}, bf16[2,28,16,128]{3,2,1,0:T(8,128)(2,1)S(1)}, bf16[28,16,128]{2,1,0:T(8,128)(2,1)S(1)}, bf16[28,16,128]{2,1,0...) custom-call(s32[2,28]{1,0:T(2,128)} %bitcast.11, ...), custom_call_target="tpu_custom_call" | custom-call | tf_op jit(solution)/shard_map/forward/pallas_call | solution.py:379
  14.6 6.4 %backward.1 = (s16[2624,128]{1,0:T(8,128)(2,1)S(1)}, f32[1808,128]{1,0:T(8,128)S(1)}) custom-call(s32[2,28]{1,0:T(2,128)} %bitcast.12, s32[63]{0:T(128)} %widths_hbm.3, s32[28]{0:T(128)} %live_hbm.1, f32[4,2,512,128]{3,2,1,0:T(8,128)S(1)} %get-tuple-element.14.planes, bf16[2,128,128]{2,1,0:T(8,128)(2,1)S(1)} %get-tuple-element.15.pupil_ref, ...), custom_call_target="tpu_custom_call" | custom-call | tf_op jit(solution)/shard_map/backward/pallas_call | solution.py:413
  21.0 15.4 %reduce_scatter.1 = (f32[2,64,512]{2,1,0:T(8,128)S(1)}, f32[2,16,128]{2,1,0:T(8,128)S(1)}) custom-call(s16[2624,128]{1,0:T(8,128)(2,1)S(1)} %get-tuple-element.22.codes, f32[1808,128]{1,0:T(8,128)S(1)} %get-tuple-element.23.floats), custom_call_target="tpu_custom_call" | custom-call | tf_op jit(solution)/shard_map/reduce_scatter/pallas_call | solution.py:524
  36.4 0.7 %copy.11 = f32[1,2,64,512]{3,2,1,0:T(8,128)} copy(f32[1,2,64,512]{3,2,1,0:T(8,128)S(1)} %bitcast.7) | data formatting | bytes 524288
  37.1 0.6 %copy.12 = f32[1,2,16,128]{3,2,1,0:T(8,128)} copy(f32[1,2,16,128]{3,2,1,0:T(8,128)S(1)} %bitcast.8) | data formatting | bytes 32768

commit v5 on v4

--- a/solution.py
+++ b/solution.py
@@ -22,18 +22,26 @@
 SPEC_ROWS = 512 // (XS * YS)
 PUP_ROWS = PUP // (XS * YS)
 CHUNKS = [(block, part) for block in range(BLOCKS) for part in range(2)]
-CHUNKS_A, CHUNKS_B = CHUNKS[:3], CHUNKS[3:]
-BOUNDS_B = [(number * SPEC_ROWS, (number + 1) * SPEC_ROWS) for number in range(len(CHUNKS_B))]
-ROWS_B = len(CHUNKS_B) * SPEC_ROWS
-BOUNDS_A = BOUNDS_B[: len(CHUNKS_A)]
-BOUNDS_A += [(len(CHUNKS_A) * SPEC_ROWS + part * PUP_ROWS, len(CHUNKS_A) * SPEC_ROWS + (part + 1) * PUP_ROWS) for part in range(2)]
-ROWS_A = len(CHUNKS_A) * SPEC_ROWS + 2 * PUP_ROWS
+SPLIT = 4
+BUNDLE_A = CHUNKS[:SPLIT]
+BUNDLE_B = CHUNKS[SPLIT:] + [(None, part) for part in range(2)]
+
+
+def bounds_of(bundle):
+    bounds, start = [], 0
+    for block, _ in bundle:
+        stop = start + (PUP_ROWS if block is None else SPEC_ROWS)
+        bounds.append((start, stop))
+        start = stop
+    return bounds
+
+
+ROWS_A, ROWS_B = bounds_of(BUNDLE_A)[-1][1], bounds_of(BUNDLE_B)[-1][1]
 SENT_A, SENT_B = 2 * (XS - 1), XS
 CODE_ROWS = SENT_A * ROWS_A + SENT_B * ROWS_B
-OWN_ROWS = 2 * ROWS_A + SENT_B * ROWS_B
-FLOAT_ROWS = OWN_ROWS + 8 * (SENT_A + SENT_B)
 LEVELS = 32767.0
 FORWARD_PAIRS = 7
+SENDS = ((0, 14),)
 PAIRS = 4
 GROUP = 2 * PAIRS
 VMEM_LIMIT = 24 * 1024 * 1024
@@ -173,9 +181,11 @@
         rows, target = strips[end]
         return remote(measured_hbm.at[:, rows], target, image_send.at[end], image_recv.at[end], other)
 
-    def edge_copy(end, other, number):
-        here = pl.ds(number * width, width)
-        return remote(edges.at[end, here], near.at[end, here], send_sems.at[end, number], recv_sems.at[end, number], other)
+    def edge_copy(end, other, number, turn):
+        here = pl.ds(number * width + SENDS[turn][0], SENDS[turn][1])
+        return remote(
+            edges.at[end, here], near.at[end, here], send_sems.at[end, number, turn], recv_sems.at[end, number, turn], other
+        )
 
     for end, present, other in sides:
         pl.when(present)(lambda: image_copy(end, other).start())
@@ -206,16 +216,19 @@
                 waves[led] = wave[:, lo : lo + PUP]
                 edges[0, led] = first[:, lo : lo + PUP]
                 edges[1, led] = last[:, lo : lo + PUP]
-        for end, present, other in sides:
-            pl.when(present)(lambda: edge_copy(end, other, number).start())
+            for turn, (low, leds) in enumerate(SENDS):
+                if 2 * (inner + 1) == low + leds:
+                    for end, present, other in sides:
+                        pl.when(present)(lambda: edge_copy(end, other, number, turn).start())
         return carry
 
     lax.fori_loop(0, steps, step, 0)
 
     def finish(number, carry):
-        for end, present, other in sides:
-            pl.when(present)(lambda: edge_copy(end, other, number).wait_send())
-            pl.when(sides[1 - end][1])(lambda: edge_copy(end, other, number).wait_recv())
+        for turn in range(len(SENDS)):
+            for end, present, other in sides:
+                pl.when(present)(lambda: edge_copy(end, other, number, turn).wait_send())
+                pl.when(sides[1 - end][1])(lambda: edge_copy(end, other, number, turn).wait_recv())
         return carry
 
     lax.fori_loop(0, steps, finish, 0)
@@ -236,7 +249,7 @@
 
 def backward_kernel(
     scale, offsets_hbm, widths_hbm, live_hbm, planes, pupil_ref, table_ref, measured_ref, above_ref, below_ref, edge_ref, waves,
-    codes, floats, spec_out, pupil_out, offsets_ref, widths_ref, live_ref, order_ref, sems
+    spec_out, pupil_out, offsets_ref, widths_ref, live_ref, order_ref, sems
 ):
     tiles = lax.axis_size("tile")
     tile = lax.axis_index("tile")
@@ -317,42 +330,6 @@
         return carry
 
     lax.fori_loop(0, steps, step, 0)
-    line, place = my_place()
-
-    def pieces_of(chunks, dest):
-        rows = pl.ds(pl.multiple_of(dest * SPEC_ROWS, SPEC_ROWS), SPEC_ROWS)
-        pieces = [spec_out[block, part, rows, :] for block, part in chunks]
-        if chunks is CHUNKS_A:
-            rows = pl.ds(pl.multiple_of(dest * PUP_ROWS, PUP_ROWS), PUP_ROWS)
-            pieces += [pupil_out[part, rows, :] for part in range(2)]
-        return pieces
-
-    code_rows, float_rows, scale_rows = [0], [0], [OWN_ROWS]
-
-    def encode(pieces):
-        for number, piece in enumerate(pieces):
-            most = jnp.maximum(jnp.max(jnp.abs(piece), axis=0, keepdims=True), 1e-30)
-            start, stop = code_rows[0], code_rows[0] + piece.shape[0]
-            codes[start:stop, :] = jnp.round(piece * (LEVELS / most)).astype(jnp.int16)
-            floats[scale_rows[0] + number : scale_rows[0] + number + 1, :] = most * (1.0 / LEVELS)
-            code_rows[0] = stop
-        scale_rows[0] += 8
-
-    def store(pieces):
-        for piece in pieces:
-            start, stop = float_rows[0], float_rows[0] + piece.shape[0]
-            floats[start:stop, :] = piece
-            float_rows[0] = stop
-
-    for turn in range(2):
-        for hop in range(XS - 1):
-            encode(pieces_of(CHUNKS_A, dest_of(line + 1 + turn, place + 1 + hop)))
-        store(pieces_of(CHUNKS_A, dest_of(line + 1 + turn, place)))
-    for hop in range(XS):
-        encode(pieces_of(CHUNKS_B, dest_of(line + 1, place + 1 + hop)))
-    for hop in range(XS):
-        store(pieces_of(CHUNKS_B, dest_of(line, place + 1 + hop)))
-
 
 def vmem():
     return pl.BlockSpec(memory_space=pltpu.VMEM)
@@ -396,8 +373,8 @@
             pltpu.SMEM(widths.shape, jnp.int32),
             pltpu.VMEM(spectrum.shape, spectrum.dtype),
             pltpu.SemaphoreType.DMA((6,)),
-            pltpu.SemaphoreType.DMA((2, chunks)),
-            pltpu.SemaphoreType.DMA((2, chunks)),
+            pltpu.SemaphoreType.DMA((2, chunks, len(SENDS))),
+            pltpu.SemaphoreType.DMA((2, chunks, len(SENDS))),
             pltpu.SemaphoreType.DMA((2,)),
             pltpu.SemaphoreType.DMA((2,)),
         ],
@@ -412,12 +389,10 @@
     lamps = measured.shape[0]
     return pl.pallas_call(
         partial(backward_kernel, scale),
-        out_shape=(pltpu.VMEM((CODE_ROWS, PUP), jnp.int16), pltpu.VMEM((FLOAT_ROWS, PUP), F32)),
+        out_shape=(pltpu.VMEM(planes.shape, F32), pltpu.VMEM(pupil.shape, F32)),
         in_specs=[hbm()] * 3 + [vmem()] * 8,
         out_specs=(vmem(), vmem()),
         scratch_shapes=[
-            pltpu.VMEM(planes.shape, F32),
-            pltpu.VMEM(pupil.shape, F32),
             pltpu.SMEM(offsets.shape, jnp.int32),
             pltpu.SMEM(widths.shape, jnp.int32),
             pltpu.SMEM(live.shape, jnp.int32),
@@ -430,7 +405,8 @@
 
 
 def gather_kernel(
-    codes, floats, spec_out, pupil_out, held, held_scales, codes2, scales2, held2, held_scales2, send_sems, recv_sems
+    spec_ref, pupil_ref, spec_out, pupil_out, codes, scales, held, held_scales, codes2, scales2, held2, held_scales2,
+    send_sems, recv_sems
 ):
     line, place = my_place()
     opposite = dest_of(line + 1, place)
@@ -438,89 +414,119 @@
     barrier = pltpu.get_barrier_semaphore()
     for other in [opposite, *beside]:
         pl.semaphore_signal(barrier, inc=1, device_id={"led": other}, device_id_type=MESH)
-    pl.semaphore_wait(barrier, XS)
+
+    def piece(block, part, dest):
+        if block is None:
+            return pupil_ref[part, pl.ds(pl.multiple_of(dest * PUP_ROWS, PUP_ROWS), PUP_ROWS), :]
+        return spec_ref[block, part, pl.ds(pl.multiple_of(dest * SPEC_ROWS, SPEC_ROWS), SPEC_ROWS), :]
+
+    def totals(bundle, dest, parts):
+        for number, ((block, part), (low, high)) in enumerate(zip(bundle, bounds_of(bundle))):
+            value = piece(block, part, dest)
+            for code, scale in parts:
+                value += code[low:high, :].astype(F32) * scale[number : number + 1, :]
+            yield number, low, high, block, part, value
+
+    def encode(bundle, dest, parts, code, scale):
+        for number, low, high, _, _, value in totals(bundle, dest, parts):
+            most = jnp.maximum(jnp.max(jnp.abs(value), axis=0, keepdims=True), 1e-30)
+            code[low:high, :] = jnp.round(value * (LEVELS / most)).astype(jnp.int16)
+            scale[number : number + 1, :] = most * (1.0 / LEVELS)
+
+    def finish(bundle, parts):
+        for _, _, _, block, part, value in totals(bundle, mine, parts):
+            if block is None:
+                pupil_out[part] = value
+            else:
+                spec_out[part, :, block * PUP : (block + 1) * PUP] = value
+
+    def first_rows(number):
+        if number < SENT_A:
+            return pl.ds(number * ROWS_A, ROWS_A)
+        return pl.ds(SENT_A * ROWS_A + (number - SENT_A) * ROWS_B, ROWS_B)
+
+    def second_rows(number):
+        return pl.ds(0, ROWS_A) if number == 0 else pl.ds(ROWS_A + (number - 1) * ROWS_B, ROWS_B)
+
     used = [0]
 
-    def send(code, scale, targets, other):
+    def send(number, rows, other, code, scale, held_code, held_scale):
         pair = []
-        for src, dst in zip((code, scale), targets):
-            number = used[0]
+        here = pl.ds(8 * number, 8)
+        targets = held_code.at[rows], held_scale.at[here]
+        for src, dst in zip((code.at[rows], scale.at[here]), targets):
+            sem = used[0]
             used[0] += 1
             pair.append(
                 pltpu.make_async_remote_copy(
-                    src_ref=src, dst_ref=dst, send_sem=send_sems.at[number], recv_sem=recv_sems.at[number],
+                    src_ref=src, dst_ref=dst, send_sem=send_sems.at[sem], recv_sem=recv_sems.at[sem],
                     device_id={"led": other}, device_id_type=MESH,
                 )
             )
             pair[-1].start()
         return pair, targets
 
-    def arrive(message):
+    def arrive(message, sent=False):
         for copy in message[0]:
-            copy.wait()
+            if not sent:
+                copy.wait_send()
+            copy.wait_recv()
         return message[1]
 
     def first(number, other):
-        rows = ROWS_A if number < SENT_A else ROWS_B
-        start = number * ROWS_A if number < SENT_A else SENT_A * ROWS_A + (number - SENT_A) * ROWS_B
-        here, scale = pl.ds(start, rows), pl.ds(8 * number, 8)
-        source_scale = pl.ds(OWN_ROWS + 8 * number, 8)
-        return send(codes.at[here], floats.at[source_scale], (held.at[here], held_scales.at[scale]), other)
+        return send(number, first_rows(number), other, codes, scales, held, held_scales)
 
     def second(number, other):
-        here, scale = second_rows(number), pl.ds(8 * number, 8)
-        return send(codes2.at[here], scales2.at[scale], (held2.at[here], held_scales2.at[scale]), other)
-
-    def second_rows(number):
-        return pl.ds(0, ROWS_A) if number == 0 else pl.ds(ROWS_A + (number - 1) * ROWS_B, ROWS_B)
-
-    def total(start, parts, number, bounds):
-        value = floats[start + bounds[0] : start + bounds[1], :]
-        for code, scale in parts:
-            value += code[bounds[0] : bounds[1], :].astype(F32) * scale[number : number + 1, :]
-        return value
-
-    def encode(start, parts, bounds, number):
-        code, scale = codes2.at[second_rows(number)], scales2.at[pl.ds(8 * number, 8)]
-        for index, (low, high) in enumerate(bounds):
-            value = total(start, parts, index, (low, high))
-            most = jnp.maximum(jnp.max(jnp.abs(value), axis=0, keepdims=True), 1e-30)
-            code[low:high, :] = jnp.round(value * (LEVELS / most)).astype(jnp.int16)
-            scale[index : index + 1, :] = most * (1.0 / LEVELS)
-
-    hops = range(XS - 1)
-    start_b = 2 * ROWS_A
-    first_b, first_a, last_a, second_b = [], [], [], []
+        return send(number, second_rows(number), other, codes2, scales2, held2, held_scales2)
+
+    hops = (1, 0, 2)
+    mine = dest_of(line, place)
+
+    def encode_first(number, bundle, dest):
+        encode(bundle, dest, [], codes.at[first_rows(number)], scales.at[pl.ds(8 * number, 8)])
+
     for hop in hops:
-        first_b.append(first(SENT_A + hop, opposite))
-        first_a.append(first(hop, beside[hop]))
-    first_b.append(first(SENT_A + XS - 1, opposite))
+        encode_first(SENT_A + hop, BUNDLE_B, dest_of(line + 1, place + 1 + hop))
+        encode_first(hop, BUNDLE_A, dest_of(line + 1, place + 1 + hop))
     for hop in hops:
-        if hop == XS - 2:
-            encode(0, [arrive(message) for message in first_a], BOUNDS_A, 0)
-            second_a = second(0, opposite)
-        encode(start_b + hop * ROWS_B, [arrive(first_b[hop])], BOUNDS_B, 1 + hop)
-        second_b.append(second(1 + hop, beside[hop]))
-        last_a.append(first(XS - 1 + hop, beside[hop]))
-
-    def put(chunks, number, value):
-        if number < len(chunks):
-            block, part = chunks[number]
-            spec_out[part, :, block * PUP : (block + 1) * PUP] = value
-        else:
-            pupil_out[number - len(chunks)] = value
-
-    parts = [arrive(first_b[XS - 1]), *(arrive(message) for message in second_b)]
-    for number, bounds in enumerate(BOUNDS_B):
-        put(CHUNKS_B, number, total(start_b + (XS - 1) * ROWS_B, parts, number, bounds))
-    parts = [*(arrive(message) for message in last_a), arrive(second_a)]
-    for number, bounds in enumerate(BOUNDS_A):
-        put(CHUNKS_A, number, total(ROWS_A, parts, number, bounds))
-
-
-def gather_call(codes, floats):
+        encode_first(XS - 1 + hop, BUNDLE_A, beside[hop])
+    encode_first(SENT_A + XS - 1, BUNDLE_B, opposite)
+    pl.semaphore_wait(barrier, XS)
+
+    first_b, first_a, last_a, second_b = {}, {}, {}, {}
+    for hop in hops:
+        first_b[hop] = first(SENT_A + hop, opposite)
+        first_a[hop] = first(hop, beside[hop])
+    last_b = first(SENT_A + XS - 1, opposite)
+    for hop in hops:
+        for copy in first_a[hop][0]:
+            copy.wait_send()
+    for hop in hops:
+        last_a[hop] = first(XS - 1 + hop, beside[hop])
+
+    def pass_on(hop):
+        parts = [arrive(first_b[hop])]
+        encode(BUNDLE_B, beside[hop], parts, codes2.at[second_rows(1 + hop)], scales2.at[pl.ds(8 * (1 + hop), 8)])
+        second_b[hop] = second(1 + hop, beside[hop])
+
+    pass_on(hops[0])
+    parts = [arrive(first_a[hop], sent=True) for hop in hops]
+    encode(BUNDLE_A, opposite, parts, codes2.at[second_rows(0)], scales2.at[pl.ds(0, 8)])
+    second_a = second(0, opposite)
+    pass_on(hops[1])
+    pass_on(hops[2])
+    parts = [*(arrive(last_a[hop]) for hop in hops), arrive(second_a)]
+    finish(BUNDLE_A, parts)
+    parts = [arrive(last_b), *(arrive(second_b[hop]) for hop in hops)]
+    finish(BUNDLE_B, parts)
+
+
+def gather_call(spec_part, pupil_part):
     moved = 2 * (SENT_A + SENT_B + XS)
-    second = (ROWS_A + (XS - 1) * ROWS_B, PUP)
+    code = pltpu.VMEM((CODE_ROWS, PUP), jnp.int16)
+    scale = pltpu.VMEM((8 * (SENT_A + SENT_B), PUP), F32)
+    code2 = pltpu.VMEM((ROWS_A + (XS - 1) * ROWS_B, PUP), jnp.int16)
+    scale2 = pltpu.VMEM((8 * XS, PUP), F32)
     return pl.pallas_call(
         gather_kernel,
         out_shape=(
@@ -530,12 +536,8 @@
         in_specs=[vmem()] * 2,
         out_specs=(vmem(), vmem()),
         scratch_shapes=[
-            pltpu.VMEM((CODE_ROWS, PUP), jnp.int16),
-            pltpu.VMEM((8 * (SENT_A + SENT_B), PUP), F32),
-            pltpu.VMEM(second, jnp.int16),
-            pltpu.VMEM((8 * XS, PUP), F32),
-            pltpu.VMEM(second, jnp.int16),
-            pltpu.VMEM((8 * XS, PUP), F32),
+            *(code, scale, code, scale),
+            *(code2, scale2, code2, scale2),
             pltpu.SemaphoreType.DMA((moved,)),
             pltpu.SemaphoreType.DMA((moved,)),
         ],
@@ -543,7 +545,33 @@
             collective_id=2, has_side_effects=True, vmem_limit_bytes=VMEM_LIMIT
         ),
         name="reduce_scatter",
-    )(*in_vmem(codes, floats))
+    )(*in_vmem(spec_part, pupil_part))
+
+
+def store_kernel(spec_ref, pupil_ref, spec_out, pupil_out, sems):
+    copies = [
+        pltpu.make_async_copy(spec_ref, spec_out, sems.at[0]),
+        pltpu.make_async_copy(pupil_ref, pupil_out, sems.at[1]),
+    ]
+    for copy in copies:
+        copy.start()
+    for copy in copies:
+        copy.wait()
+
+
+def store_call(spec_share, pupil_share):
+    return pl.pallas_call(
+        store_kernel,
+        out_shape=(
+            jax.ShapeDtypeStruct(spec_share.shape, F32),
+            jax.ShapeDtypeStruct(pupil_share.shape, F32),
+        ),
+        in_specs=[vmem()] * 2,
+        out_specs=(hbm(), hbm()),
+        scratch_shapes=[pltpu.SemaphoreType.DMA((2,))],
+        compiler_params=pltpu.CompilerParams(vmem_limit_bytes=VMEM_LIMIT),
+        name="store",
+    )(*in_vmem(spec_share, pupil_share))
 
 
 def on_device(tables, spectrum, pupil, offsets, widths, live, measured):
@@ -557,7 +585,7 @@
     parts = backward_call(
         scale, offsets, widths, live, planes, pupil, tables, measured, above, below, near, waves
     )
-    spec_share, pupil_share = gather_call(*parts)
+    spec_share, pupil_share = store_call(*gather_call(*parts))
     return spec_share[None], pupil_share[None]
 
 

time: 38.1 us -> 35.6 us (0.934)
  local copies, waits for them, and re-layouts: 1.31 us -> 0 us
  Pallas kernels: 35.7 us -> 34.8 us
    unnamed x2 -> x0, local copies, waits for them, and re-layouts: 1.31 us -> none
    pallas_call x1, Pallas kernels: 15.4 us -> 14.2 us  [gather_call(): pl.pallas_call(gather_kernel, out_shape=(pltpu.VMEM((2, SPEC_ROWS, BLOCKS...]
    pallas_call x1 -> x2, Pallas kernels: 6.4 us -> 6.68 us  [the longest x1 5.95 us: backward_call(): pl.pallas_call(partial(backward_kernel, scale), out_shape=(pltpu.VMEM(pla...]
where the time goes in v5:
time: 35.6 us; the launch traced here: 35.4 us
  Pallas kernels  34.8 us (98%)
  between operations  0.65 us (2%)
    pallas_call x1, Pallas kernels, gather_call(): pl.pallas_call(gather_kernel, out_shape=(pltpu.VMEM((2, SPEC_ROWS, BLOCKS...  14.2 us
    pallas_call x1, Pallas kernels, forward_call(): pl.pallas_call(forward_kernel, out_shape=(pltpu.VMEM((lamps, 2 * PUP, PUP...  13.9 us
    pallas_call x1, Pallas kernels, backward_call(): pl.pallas_call(partial(backward_kernel, scale), out_shape=(pltpu.VMEM(pla...  5.95 us
    pallas_call x1, Pallas kernels, store_call(): pl.pallas_call(store_kernel, out_shape=(jax.ShapeDtypeStruct(spec_share.s...  0.72 us

profile of v5, /device:TPU:1, one launch (start us, length us, event | category | flops | bytes accessed | tf_op | source)
XLA Modules:
  0.0 35.4 jit_solution(4304181289436822216)
XLA Ops:
  0.6 13.9 %forward.1 = (f32[28,256,128]{2,1,0:T(8,128)S(1)}, bf16[2,28,16,128]{3,2,1,0:T(8,128)(2,1)S(1)}, bf16[28,16,128]{2,1,0:T(8,128)(2,1)S(1)}, bf16[28,16,128]{2,1,0...) custom-call(s32[2,28]{1,0:T(2,128)} %bitcast.9, ...), custom_call_target="tpu_custom_call" | custom-call | tf_op jit(solution)/shard_map/forward/pallas_call | solution.py:356
  14.6 6.0 %backward.1 = (f32[4,2,512,128]{3,2,1,0:T(8,128)S(1)}, f32[2,128,128]{2,1,0:T(8,128)S(1)}) custom-call(s32[2,28]{1,0:T(2,128)} %bitcast.10, s32[63]{0:T(128)} %widths_hbm.3, s32[28]{0:T(128)} %live_hbm.1, f32[4,2,512,128]{3,2,1,0:T(8,128)S(1)} %get-tuple-element.16.planes, bf16[2,128,128]{2,1,0:T(8,128)(2,1)S(1)} %get-tuple-element.17.pupil_ref, ...), custom_call_target="tpu_custom_call" | custom-call | tf_op jit(solution)/shard_map/backward/pallas_call | solution.py:390
  20.5 14.2 %reduce_scatter.1 = (f32[2,64,512]{2,1,0:T(8,128)S(1)}, f32[2,16,128]{2,1,0:T(8,128)S(1)}) custom-call(f32[4,2,512,128]{3,2,1,0:T(8,128)S(1)} %get-tuple-element.24.spec_ref, f32[2,128,128]{2,1,0:T(8,128)S(1)} %get-tuple-element.25.pupil_ref), custom_call_target="tpu_custom_call" | custom-call | tf_op jit(solution)/shard_map/reduce_scatter/pallas_call | solution.py:530
  34.7 0.7 %store.1 = (f32[2,64,512]{2,1,0:T(8,128)}, f32[2,16,128]{2,1,0:T(8,128)}) custom-call(f32[2,64,512]{2,1,0:T(8,128)S(1)} %get-tuple-element.26.spec_ref, f32[2,16,128]{2,1,0:T(8,128)S(1)} %get-tuple-element.27.pupil_ref), custom_call_target="tpu_custom_call" | custom-call | tf_op jit(solution)/shard_map/store/pallas_call | solution.py:563

commit v6 on v5

--- a/solution.py
+++ b/solution.py
@@ -23,8 +23,8 @@
 PUP_ROWS = PUP // (XS * YS)
 CHUNKS = [(block, part) for block in range(BLOCKS) for part in range(2)]
 SPLIT = 4
-BUNDLE_A = CHUNKS[:SPLIT]
-BUNDLE_B = CHUNKS[SPLIT:] + [(None, part) for part in range(2)]
+BUNDLE_A = CHUNKS[:SPLIT] + [(None, part) for part in range(2)]
+BUNDLE_B = CHUNKS[SPLIT:]
 
 
 def bounds_of(bundle):
@@ -42,7 +42,7 @@
 LEVELS = 32767.0
 FORWARD_PAIRS = 7
 SENDS = ((0, 14),)
-PAIRS = 4
+PAIRS = 6
 GROUP = 2 * PAIRS
 VMEM_LIMIT = 24 * 1024 * 1024
 
@@ -68,9 +68,8 @@
 
 def right_product(x, high, low):
     xh, xl = split(x)
-    data = jnp.concatenate([xh, xl, xh], axis=1)
-    table = jnp.concatenate([high, high, low], axis=0)
-    return jnp.dot(data, table, preferred_element_type=F32)
+    product = partial(jnp.dot, preferred_element_type=F32)
+    return product(xh, high) + product(xl, high) + product(xh, low)
 
 
 def left_product(high, low, x):
@@ -108,10 +107,9 @@
     return count
 
 
-def load_spectrum(spec_ref, planes):
+def load_spectrum(spec_ref, planes, part):
     for block in range(BLOCKS):
-        for part in range(2):
-            planes[block, part] = spec_ref[part, :, block * PUP : (block + 1) * PUP].astype(F32)
+        planes[block, part] = spec_ref[part, :, block * PUP : (block + 1) * PUP].astype(F32)
 
 
 def window_of(planes, row, col):
@@ -126,9 +124,9 @@
 
 
 def forward_kernel(
-    offsets_hbm, widths_hbm, spec_hbm, pupil_hbm, table_hbm, measured_hbm,
-    waves, near, above, below, planes, pupil_ref, table_ref, measured_ref,
-    edges, offsets_ref, widths_ref, spec_ref, local_sems, send_sems, recv_sems, image_send, image_recv
+    offsets_hbm, widths_hbm, live_hbm, spec_hbm, pupil_hbm, table_hbm, measured_hbm,
+    waves, near, above, below, planes, pupil_ref, table_ref, measured_ref, offsets_ref, widths_ref, live_ref,
+    edges, spec_ref, local_sems, send_sems, recv_sems, image_send, image_recv
 ):
     tiles = lax.axis_size("tile")
     tile = lax.axis_index("tile")
@@ -141,14 +139,16 @@
             (
                 (offsets_hbm, offsets_ref),
                 (widths_hbm, widths_ref),
-                (spec_hbm, spec_ref),
+                (live_hbm, live_ref),
+                (spec_hbm.at[0], spec_ref.at[0]),
+                (spec_hbm.at[1], spec_ref.at[1]),
                 (pupil_hbm, pupil_ref),
                 (table_hbm, table_ref),
                 (measured_hbm, measured_ref),
             )
         )
     ]
-    for copy in local:
+    for copy in local[:-1]:
         copy.start()
     barrier = pltpu.get_barrier_semaphore()
     has_above, has_below = tile > 0, tile < tiles - 1
@@ -158,13 +158,16 @@
 
     pl.when(has_above)(lambda: signal(up))
     pl.when(has_below)(lambda: signal(down))
+    for part in range(2):
+        local[3 + part].wait()
+        load_spectrum(spec_ref, planes, part)
+    local[-1].start()
     for copy in local[:3]:
         copy.wait()
-    load_spectrum(spec_ref, planes)
     top, bottom = ramp_weights(widths_ref, tile, tiles)
     top2 = jnp.concatenate([top, top], axis=1)
     bottom2 = jnp.concatenate([bottom, bottom], axis=1)
-    for copy in local[3:5]:
+    for copy in local[5:-1]:
         copy.wait()
     pl.semaphore_wait(barrier, has_above.astype(jnp.int32) + has_below.astype(jnp.int32))
 
@@ -232,7 +235,7 @@
         return carry
 
     lax.fori_loop(0, steps, finish, 0)
-    local[5].wait()
+    local[-1].wait()
     for end, present, other in sides:
         pl.when(present)(lambda: image_copy(end, other).wait_send())
         pl.when(sides[1 - end][1])(lambda: image_copy(end, other).wait_recv())
@@ -248,23 +251,13 @@
 
 
 def backward_kernel(
-    scale, offsets_hbm, widths_hbm, live_hbm, planes, pupil_ref, table_ref, measured_ref, above_ref, below_ref, edge_ref, waves,
-    spec_out, pupil_out, offsets_ref, widths_ref, live_ref, order_ref, sems
+    scale, offsets_ref, widths_ref, live_ref, planes, pupil_ref, table_ref, measured_ref, above_ref, below_ref, edge_ref, waves,
+    spec_out, pupil_out, order_ref
 ):
     tiles = lax.axis_size("tile")
     tile = lax.axis_index("tile")
-    local = [
-        pltpu.make_async_copy(source, target, sems.at[number])
-        for number, (source, target) in enumerate(
-            ((offsets_hbm, offsets_ref), (widths_hbm, widths_ref), (live_hbm, live_ref))
-        )
-    ]
-    for copy in local:
-        copy.start()
     spec_out[...] = jnp.zeros_like(spec_out)
     pupil_out[...] = jnp.zeros_like(pupil_out)
-    for copy in local:
-        copy.wait()
     count = list_live(live_ref, order_ref)
     steps = (count + GROUP - 1) // GROUP
 
@@ -335,6 +328,10 @@
     return pl.BlockSpec(memory_space=pltpu.VMEM)
 
 
+def smem():
+    return pl.BlockSpec(memory_space=pltpu.SMEM)
+
+
 def hbm():
     return pl.BlockSpec(memory_space=pltpu.HBM)
 
@@ -343,11 +340,15 @@
     return [pltpu.with_memory_space_constraint(array, pltpu.HBM) for array in arrays]
 
 
+def in_smem(*arrays):
+    return [pltpu.with_memory_space_constraint(array, pltpu.SMEM) for array in arrays]
+
+
 def in_vmem(*arrays):
     return [pltpu.with_memory_space_constraint(array, pltpu.VMEM) for array in arrays]
 
 
-def forward_call(offsets, widths, spectrum, pupil, tables, measured):
+def forward_call(offsets, widths, live, spectrum, pupil, tables, measured):
     lamps = measured.shape[0]
     side = spectrum.shape[-1]
     rows = pltpu.VMEM((lamps, OV, PUP), measured.dtype)
@@ -364,15 +365,16 @@
             pltpu.VMEM(pupil.shape, pupil.dtype),
             pltpu.VMEM(tables.shape, tables.dtype),
             pltpu.VMEM(measured.shape, measured.dtype),
+            pltpu.SMEM(offsets.shape, jnp.int32),
+            pltpu.SMEM(widths.shape, jnp.int32),
+            pltpu.SMEM(live.shape, jnp.int32),
         ),
-        in_specs=[hbm()] * 6,
-        out_specs=(vmem(),) * 8,
+        in_specs=[hbm()] * 7,
+        out_specs=(vmem(),) * 8 + (smem(),) * 3,
         scratch_shapes=[
             edge,
-            pltpu.SMEM(offsets.shape, jnp.int32),
-            pltpu.SMEM(widths.shape, jnp.int32),
             pltpu.VMEM(spectrum.shape, spectrum.dtype),
-            pltpu.SemaphoreType.DMA((6,)),
+            pltpu.SemaphoreType.DMA((8,)),
             pltpu.SemaphoreType.DMA((2, chunks, len(SENDS))),
             pltpu.SemaphoreType.DMA((2, chunks, len(SENDS))),
             pltpu.SemaphoreType.DMA((2,)),
@@ -382,7 +384,7 @@
             collective_id=1, has_side_effects=True, vmem_limit_bytes=VMEM_LIMIT
         ),
         name="forward",
-    )(*in_hbm(offsets, widths, spectrum, pupil, tables, measured))
+    )(*in_hbm(offsets, widths, live, spectrum, pupil, tables, measured))
 
 
 def backward_call(scale, offsets, widths, live, planes, pupil, tables, measured, above, below, edges, waves):
@@ -390,18 +392,12 @@
     return pl.pallas_call(
         partial(backward_kernel, scale),
         out_shape=(pltpu.VMEM(planes.shape, F32), pltpu.VMEM(pupil.shape, F32)),
-        in_specs=[hbm()] * 3 + [vmem()] * 8,
+        in_specs=[smem()] * 3 + [vmem()] * 8,
         out_specs=(vmem(), vmem()),
-        scratch_shapes=[
-            pltpu.SMEM(offsets.shape, jnp.int32),
-            pltpu.SMEM(widths.shape, jnp.int32),
-            pltpu.SMEM(live.shape, jnp.int32),
-            pltpu.SMEM((lamps + GROUP,), jnp.int32),
-            pltpu.SemaphoreType.DMA((3,)),
-        ],
+        scratch_shapes=[pltpu.SMEM((lamps + GROUP,), jnp.int32)],
         compiler_params=pltpu.CompilerParams(vmem_limit_bytes=VMEM_LIMIT),
         name="backward",
-    )(*in_hbm(offsets, widths, live), *in_vmem(planes, pupil, tables, measured, above, below, edges, waves))
+    )(*in_smem(offsets, widths, live), *in_vmem(planes, pupil, tables, measured, above, below, edges, waves))
 
 
 def gather_kernel(
@@ -454,7 +450,7 @@
         pair = []
         here = pl.ds(8 * number, 8)
         targets = held_code.at[rows], held_scale.at[here]
-        for src, dst in zip((code.at[rows], scale.at[here]), targets):
+        for src, dst in zip((scale.at[here], code.at[rows]), reversed(targets)):
             sem = used[0]
             used[0] += 1
             pair.append(
@@ -579,8 +575,8 @@
     lamps = measured.shape[0]
     scale = 1.0 / math.sqrt(lamps * groups)
     spectrum, pupil, offsets = spectrum[0], pupil[0], offsets[0].T
-    waves, near, above, below, planes, pupil, tables, measured = forward_call(
-        offsets, widths, spectrum, pupil, tables, measured
+    waves, near, above, below, planes, pupil, tables, measured, offsets, widths, live = forward_call(
+        offsets, widths, live, spectrum, pupil, tables, measured
     )
     parts = backward_call(
         scale, offsets, widths, live, planes, pupil, tables, measured, above, below, near, waves

time: 35.6 us -> 34.9 us (0.980)
  Pallas kernels: 34.8 us -> 34.1 us
    pallas_call x1, Pallas kernels: 5.95 us -> 4.89 us  [backward_call(): pl.pallas_call(partial(backward_kernel, scale), out_shape=(pltpu.VMEM(pla...]
    pallas_call x1, Pallas kernels: 14.2 us -> 14.5 us  [gather_call(): pl.pallas_call(gather_kernel, out_shape=(pltpu.VMEM((2, SPEC_ROWS, BLOCKS...]
where the time goes in v6:
time: 34.9 us; the launch traced here: 34.7 us
  Pallas kernels  34.1 us (98%)
  between operations  0.65 us (2%)
    pallas_call x1, Pallas kernels, gather_call(): pl.pallas_call(gather_kernel, out_shape=(pltpu.VMEM((2, SPEC_ROWS, BLOCKS...  14.5 us
    pallas_call x1, Pallas kernels, forward_call(): pl.pallas_call(forward_kernel, out_shape=(pltpu.VMEM((lamps, 2 * PUP, PUP...  13.9 us
    pallas_call x1, Pallas kernels, backward_call(): pl.pallas_call(partial(backward_kernel, scale), out_shape=(pltpu.VMEM(pla...  4.89 us
    pallas_call x1, Pallas kernels, store_call(): pl.pallas_call(store_kernel, out_shape=(jax.ShapeDtypeStruct(spec_share.s...  0.72 us

profile of v6, /device:TPU:1, one launch (start us, length us, event | category | flops | bytes accessed | tf_op | source)
XLA Modules:
  0.0 34.7 jit_solution(879910043354723875)
XLA Ops:
  0.6 13.9 %forward.1 = (f32[28,256,128]{2,1,0:T(8,128)S(1)}, bf16[2,28,16,128]{3,2,1,0:T(8,128)(2,1)S(1)}, bf16[28,16,128]{2,1,0:T(8,128)(2,1)S(1)}, bf16[28,16,128]{2,1,0...) custom-call(s32[2,28]{1,0:T(2,128)} %bitcast.9, ...), custom_call_target="tpu_custom_call" | custom-call | tf_op jit(solution)/shard_map/forward/pallas_call | solution.py:357
  14.5 4.9 %backward.1 = (f32[4,2,512,128]{3,2,1,0:T(8,128)S(1)}, f32[2,128,128]{2,1,0:T(8,128)S(1)}) custom-call(s32[2,28]{1,0:T(2,128)S(4)} %get-tuple-element.19.offsets_ref, s32[63]{0:T(128)S(4)} %get-tuple-element.20.widths_ref, s32[28]{0:T(128)S(4)} %get-tuple-element.21.live_ref, f32[4,2,512,128]{3,2,1,0:T(8,128)S(1)} %get-tuple-element.22.planes, ...), custom_call_target="tpu_custom_call" | custom-call | tf_op jit(solution)/shard_map/backward/pallas_call | solution.py:392
  19.4 14.5 %reduce_scatter.1 = (f32[2,64,512]{2,1,0:T(8,128)S(1)}, f32[2,16,128]{2,1,0:T(8,128)S(1)}) custom-call(f32[4,2,512,128]{3,2,1,0:T(8,128)S(1)} %get-tuple-element.30.spec_ref, f32[2,128,128]{2,1,0:T(8,128)S(1)} %get-tuple-element.31.pupil_ref), custom_call_target="tpu_custom_call" | custom-call | tf_op jit(solution)/shard_map/reduce_scatter/pallas_call | solution.py:526
  34.0 0.7 %store.1 = (f32[2,64,512]{2,1,0:T(8,128)}, f32[2,16,128]{2,1,0:T(8,128)}) custom-call(f32[2,64,512]{2,1,0:T(8,128)S(1)} %get-tuple-element.32.spec_ref, f32[2,16,128]{2,1,0:T(8,128)S(1)} %get-tuple-element.33.pupil_ref), custom_call_target="tpu_custom_call" | custom-call | tf_op jit(solution)/shard_map/store/pallas_call | solution.py:559

commit v7 on v6

--- a/solution.py
+++ b/solution.py
@@ -14,6 +14,7 @@
 OV = 16
 HALF = 8
 STRIDE = PUP - OV
+INNER = STRIDE - OV
 BLOCKS = 4
 MESH = pl.DeviceIdType.MESH
 F32 = jnp.float32
@@ -72,8 +73,7 @@
     return product(xh, high) + product(xl, high) + product(xh, low)
 
 
-def left_product(high, low, x):
-    xh, xl = split(x)
+def left_product(high, low, xh, xl):
     data = jnp.concatenate([xh, xl, xh], axis=0)
     table = jnp.concatenate([high, high, low], axis=1)
     return jnp.dot(table, data, preferred_element_type=F32)
@@ -103,7 +103,7 @@
     lamps = live_ref.shape[0]
     count = lax.fori_loop(0, lamps, body, jnp.int32(0))
     for extra in range(GROUP):
-        order_ref[count + extra] = 0
+        order_ref[count + extra] = lamps
     return count
 
 
@@ -124,9 +124,10 @@
 
 
 def forward_kernel(
+    scale,
     offsets_hbm, widths_hbm, live_hbm, spec_hbm, pupil_hbm, table_hbm, measured_hbm,
-    waves, near, above, below, planes, pupil_ref, table_ref, measured_ref, offsets_ref, widths_ref, live_ref,
-    edges, spec_ref, local_sems, send_sems, recv_sems, image_send, image_recv
+    middle, ends, near, above, below, planes, pupil_ref, table_ref, measured_ref, offsets_ref, widths_ref, live_ref,
+    waves, edges, spec_ref, local_sems, send_sems, recv_sems, image_send, image_recv
 ):
     tiles = lax.axis_size("tile")
     tile = lax.axis_index("tile")
@@ -208,7 +209,7 @@
             pair = number * FORWARD_PAIRS + inner
             field = jnp.concatenate([field_of(2 * pair), field_of(2 * pair + 1)], axis=0)
             mixed = right_product(field, table_ref[0], table_ref[1])
-            wave = left_product(table_ref[2], table_ref[3], swap_blocks(mixed))
+            wave = left_product(table_ref[2], table_ref[3], *split(swap_blocks(mixed)))
             first = wave[:OV], wave[PUP : PUP + OV]
             last = wave[STRIDE:PUP], wave[PUP + STRIDE :]
             first = (top2 * (first[0] * first[0] + first[1] * first[1])).astype(BF16)
@@ -217,6 +218,9 @@
                 lo = side * PUP
                 led = 2 * pair + side
                 waves[led] = wave[:, lo : lo + PUP]
+                for part in range(2):
+                    ends[led, part, :OV] = wave[part * PUP : part * PUP + OV, lo : lo + PUP]
+                    ends[led, part, OV:] = wave[part * PUP + STRIDE : (part + 1) * PUP, lo : lo + PUP]
                 edges[0, led] = first[:, lo : lo + PUP]
                 edges[1, led] = last[:, lo : lo + PUP]
             for turn, (low, leds) in enumerate(SENDS):
@@ -226,6 +230,30 @@
         return carry
 
     lax.fori_loop(0, steps, step, 0)
+    local[-1].wait()
+
+    def inner_rows(led):
+        rows = [waves[led, part * PUP + OV : part * PUP + STRIDE] for part in range(2)]
+        seen = measured_ref[led].astype(F32)[HALF : STRIDE - HALF]
+        grad = (2.0 * scale) * (rows[0] * rows[0] + rows[1] * rows[1] - seen)
+        return jnp.concatenate([grad * rows[0], grad * rows[1]], axis=1)
+
+    def inner_step(number, carry):
+        for inner in range(FORWARD_PAIRS):
+            leds = [2 * (number * FORWARD_PAIRS + inner) + side for side in range(2)]
+            rows = jnp.concatenate([inner_rows(led) for led in leds], axis=0)
+            for kind, value in enumerate(split(right_product(rows, table_ref[2], table_ref[3]))):
+                for side, led in enumerate(leds):
+                    for part in range(2):
+                        middle[kind, led, part] = value[side * INNER : (side + 1) * INNER, part * PUP : (part + 1) * PUP]
+        return carry
+
+    lax.fori_loop(0, steps, inner_step, 0)
+    lamps = waves.shape[0]
+    for part in range(2):
+        ends[lamps, part] = jnp.zeros((2 * OV, PUP), F32)
+        for kind in range(2):
+            middle[kind, lamps, part] = jnp.zeros((INNER, PUP), BF16)
 
     def finish(number, carry):
         for turn in range(len(SENDS)):
@@ -235,7 +263,6 @@
         return carry
 
     lax.fori_loop(0, steps, finish, 0)
-    local[-1].wait()
     for end, present, other in sides:
         pl.when(present)(lambda: image_copy(end, other).wait_send())
         pl.when(sides[1 - end][1])(lambda: image_copy(end, other).wait_recv())
@@ -251,7 +278,7 @@
 
 
 def backward_kernel(
-    scale, offsets_ref, widths_ref, live_ref, planes, pupil_ref, table_ref, measured_ref, above_ref, below_ref, edge_ref, waves,
+    scale, offsets_ref, widths_ref, live_ref, planes, pupil_ref, table_ref, measured_ref, above_ref, below_ref, edge_ref, middle, ends,
     spec_out, pupil_out, order_ref
 ):
     tiles = lax.axis_size("tile")
@@ -271,38 +298,68 @@
     has_below = tile < tiles - 1
     lanes = lax.broadcasted_iota(jnp.int32, (PUP, PUP), 1)
 
-    def edges_of(end, leds):
-        return jnp.concatenate([edge_ref[end, led].astype(F32) for led in leds], axis=1)
-
-    def images(ref, leds, low, high):
-        return jnp.concatenate([ref[led, low:high].astype(F32) for led in leds], axis=1)
+    lamps = measured_ref.shape[0]
+
+    def spots_of(leds):
+        return [jnp.minimum(led, lamps - 1) for led in leds]
+
+    def edges_of(end, spots):
+        return jnp.concatenate([edge_ref[end, spot].astype(F32) for spot in spots], axis=1)
+
+    def images(ref, spots, low, high):
+        return jnp.concatenate([ref[spot, low:high].astype(F32) for spot in spots], axis=1)
+
+    def end_rows(leds):
+        spots = spots_of(leds)
+        wave = [jnp.concatenate([ends[led, part] for led in leds], axis=1) for part in range(2)]
+        intensity = wave[0] * wave[0] + wave[1] * wave[1]
+        upper = images(above_ref, spots, OV - HALF, OV)
+        lower = images(below_ref, spots, 0, HALF)
+        own_top = images(measured_ref, spots, 0, OV)[: OV - HALF]
+        own_bottom = images(measured_ref, spots, STRIDE - OV, STRIDE)[OV - HALF :]
+        near_top = jnp.where(has_above, edges_of(1, spots), 0.0)
+        near_bottom = jnp.where(has_below, edges_of(0, spots), 0.0)
+        first = top2 * (top2 * intensity[:OV] + near_top - jnp.concatenate([upper, own_top], axis=0))
+        last = bottom2 * (bottom2 * intensity[OV:] + near_bottom - jnp.concatenate([own_bottom, lower], axis=0))
+        grad = (2.0 * scale) * jnp.concatenate(
+            [jnp.where(top_inside, first, 0.0), jnp.where(bottom_inside, last, 0.0)], axis=0
+        )
+        grad_wave = [grad * wave[part] for part in range(2)]
+        return [
+            jnp.concatenate([grad_wave[part][:, side * PUP : (side + 1) * PUP] for part in range(2)], axis=1)
+            for side in range(2)
+        ]
 
     def step(number, carry):
-        for inner in range(PAIRS):
-            pair = number * PAIRS + inner
-            leds = order_ref[2 * pair], order_ref[2 * pair + 1]
-            side_of = lax.broadcasted_iota(jnp.int32, (1, 2 * PUP), 1) // PUP
-            alive = jnp.where(2 * pair + side_of < count, scale, 0.0)
-            wave = jnp.concatenate([waves[led] for led in leds], axis=1)
-            wave_re, wave_im = wave[:PUP], wave[PUP:]
-            intensity = wave_re * wave_re + wave_im * wave_im
-            own = images(measured_ref, leds, 0, STRIDE)
-            upper = images(above_ref, leds, OV - HALF, OV)
-            lower = images(below_ref, leds, 0, HALF)
-            near_top = jnp.where(has_above, edges_of(1, leds), 0.0)
-            near_bottom = jnp.where(has_below, edges_of(0, leds), 0.0)
-            first = 2.0 * top2 * (top2 * intensity[:OV] + near_top - jnp.concatenate([upper, own[: OV - HALF]], axis=0))
-            middle = 2.0 * (intensity[OV:STRIDE] - own[HALF : STRIDE - HALF])
-            last = 2.0 * bottom2 * (bottom2 * intensity[STRIDE:] + near_bottom - jnp.concatenate([own[STRIDE - HALF :], lower], axis=0))
-            grad = alive * jnp.concatenate(
-                [jnp.where(top_inside, first, 0.0), middle, jnp.where(bottom_inside, last, 0.0)], axis=0
-            )
-            grad_wave = jnp.concatenate([grad * wave_re, grad * wave_im], axis=0)
-            back = right_product(swap_blocks(grad_wave), table_ref[2], table_ref[3])
-            grad_field = left_product(table_ref[0], table_ref[1], swap_blocks(back))
+        pairs = [
+            [order_ref[2 * (number * PAIRS + inner) + side] for side in range(2)] for inner in range(PAIRS)
+        ]
+        rows = jnp.concatenate([row for leds in pairs for row in end_rows(leds)], axis=0)
+        outer = split(right_product(rows, table_ref[2], table_ref[3]))
+        for inner, leds in enumerate(pairs):
+
+            def column(kind, side, part):
+                start = 2 * OV * (2 * inner + side)
+                lanes_of = slice(part * PUP, (part + 1) * PUP)
+                return jnp.concatenate(
+                    [
+                        outer[kind][start : start + OV, lanes_of],
+                        middle[kind, leds[side], part],
+                        outer[kind][start + OV : start + 2 * OV, lanes_of],
+                    ],
+                    axis=0,
+                )
+
+            def data(kind):
+                columns = [
+                    jnp.concatenate([column(kind, side, part) for part in range(2)], axis=0) for side in range(2)
+                ]
+                return jnp.concatenate(columns, axis=1)
+
+            grad_field = left_product(table_ref[0], table_ref[1], data(0), data(1))
+            spots = spots_of(leds)
             for side in range(2):
-                led = leds[side]
-                row, col = offsets_ref[0, led], offsets_ref[1, led]
+                row, col = offsets_ref[0, spots[side]], offsets_ref[1, spots[side]]
                 shift = col % PUP
                 lo = side * PUP
                 grad_re = grad_field[:PUP, lo : lo + PUP]
@@ -348,16 +405,17 @@
     return [pltpu.with_memory_space_constraint(array, pltpu.VMEM) for array in arrays]
 
 
-def forward_call(offsets, widths, live, spectrum, pupil, tables, measured):
+def forward_call(scale, offsets, widths, live, spectrum, pupil, tables, measured):
     lamps = measured.shape[0]
     side = spectrum.shape[-1]
     rows = pltpu.VMEM((lamps, OV, PUP), measured.dtype)
     edge = pltpu.VMEM((2, lamps, OV, PUP), BF16)
     chunks = lamps // (2 * FORWARD_PAIRS)
     return pl.pallas_call(
-        forward_kernel,
+        partial(forward_kernel, scale),
         out_shape=(
-            pltpu.VMEM((lamps, 2 * PUP, PUP), F32),
+            pltpu.VMEM((2, lamps + 1, 2, INNER, PUP), BF16),
+            pltpu.VMEM((lamps + 1, 2, 2 * OV, PUP), F32),
             edge,
             rows,
             rows,
@@ -370,8 +428,9 @@
             pltpu.SMEM(live.shape, jnp.int32),
         ),
         in_specs=[hbm()] * 7,
-        out_specs=(vmem(),) * 8 + (smem(),) * 3,
+        out_specs=(vmem(),) * 9 + (smem(),) * 3,
         scratch_shapes=[
+            pltpu.VMEM((lamps, 2 * PUP, PUP), F32),
             edge,
             pltpu.VMEM(spectrum.shape, spectrum.dtype),
             pltpu.SemaphoreType.DMA((8,)),
@@ -387,17 +446,17 @@
     )(*in_hbm(offsets, widths, live, spectrum, pupil, tables, measured))
 
 
-def backward_call(scale, offsets, widths, live, planes, pupil, tables, measured, above, below, edges, waves):
+def backward_call(scale, offsets, widths, live, planes, pupil, tables, measured, above, below, edges, middle, ends):
     lamps = measured.shape[0]
     return pl.pallas_call(
         partial(backward_kernel, scale),
         out_shape=(pltpu.VMEM(planes.shape, F32), pltpu.VMEM(pupil.shape, F32)),
-        in_specs=[smem()] * 3 + [vmem()] * 8,
+        in_specs=[smem()] * 3 + [vmem()] * 9,
         out_specs=(vmem(), vmem()),
         scratch_shapes=[pltpu.SMEM((lamps + GROUP,), jnp.int32)],
         compiler_params=pltpu.CompilerParams(vmem_limit_bytes=VMEM_LIMIT),
         name="backward",
-    )(*in_smem(offsets, widths, live), *in_vmem(planes, pupil, tables, measured, above, below, edges, waves))
+    )(*in_smem(offsets, widths, live), *in_vmem(planes, pupil, tables, measured, above, below, edges, middle, ends))
 
 
 def gather_kernel(
@@ -575,11 +634,11 @@
     lamps = measured.shape[0]
     scale = 1.0 / math.sqrt(lamps * groups)
     spectrum, pupil, offsets = spectrum[0], pupil[0], offsets[0].T
-    waves, near, above, below, planes, pupil, tables, measured, offsets, widths, live = forward_call(
-        offsets, widths, live, spectrum, pupil, tables, measured
+    middle, ends, near, above, below, planes, pupil, tables, measured, offsets, widths, live = forward_call(
+        scale, offsets, widths, live, spectrum, pupil, tables, measured
     )
     parts = backward_call(
-        scale, offsets, widths, live, planes, pupil, tables, measured, above, below, near, waves
+        scale, offsets, widths, live, planes, pupil, tables, measured, above, below, near, middle, ends
     )
     spec_share, pupil_share = store_call(*gather_call(*parts))
     return spec_share[None], pupil_share[None]

time: 34.9 us -> 33.4 us (0.957)
  Pallas kernels: 34.1 us -> 32.3 us
    pallas_call x1, Pallas kernels: 14.5 us -> 13.4 us  [gather_call(): pl.pallas_call(gather_kernel, out_shape=(pltpu.VMEM((2, SPEC_ROWS, BLOCKS...]
    pallas_call x1, Pallas kernels: 4.89 us -> 4.33 us  [backward_call(): pl.pallas_call(partial(backward_kernel, scale), out_shape=(pltpu.VMEM(pla...]
where the time goes in v7:
time: 33.4 us; the launch traced here: 33 us
  Pallas kernels  32.3 us (97%)
  between operations  0.65 us (2%)
    pallas_call x1, Pallas kernels, forward_call(): pl.pallas_call(partial(forward_kernel, scale), out_shape=(pltpu.VMEM((2,...  13.9 us
    pallas_call x1, Pallas kernels, gather_call(): pl.pallas_call(gather_kernel, out_shape=(pltpu.VMEM((2, SPEC_ROWS, BLOCKS...  13.4 us
    pallas_call x1, Pallas kernels, backward_call(): pl.pallas_call(partial(backward_kernel, scale), out_shape=(pltpu.VMEM(pla...  4.33 us
    pallas_call x1, Pallas kernels, store_call(): pl.pallas_call(store_kernel, out_shape=(jax.ShapeDtypeStruct(spec_share.s...  0.72 us

profile of v7, /device:TPU:1, one launch (start us, length us, event | category | flops | bytes accessed | tf_op | source)
XLA Modules:
  0.0 33.0 jit_solution(15083406036386318273)
XLA Ops:
  0.6 13.9 %forward.1 = (bf16[2,29,2,96,128]{4,3,2,1,0:T(8,128)(2,1)S(1)}, f32[29,2,32,128]{3,2,1,0:T(8,128)S(1)}, bf16[2,28,16,128]{3,2,1,0:T(8,128)(2,1)S(1)}, bf16[28,16...) custom-call(s32[2,28]{1,0:T(2,128)} %bitcast.9, ...), custom_call_target="tpu_custom_call" | custom-call | tf_op jit(solution)/shard_map/forward/pallas_call | solution.py:414
  14.5 4.3 %backward.1 = (f32[4,2,512,128]{3,2,1,0:T(8,128)S(1)}, f32[2,128,128]{2,1,0:T(8,128)S(1)}) custom-call(s32[2,28]{1,0:T(2,128)S(4)} %get-tuple-element.20.offsets_ref, s32[63]{0:T(128)S(4)} %get-tuple-element.21.widths_ref, s32[28]{0:T(128)S(4)} %get-tuple-element.22.live_ref, f32[4,2,512,128]{3,2,1,0:T(8,128)S(1)} %get-tuple-element.23.planes, ...), custom_call_target="tpu_custom_call" | custom-call | tf_op jit(solution)/shard_map/backward/pallas_call | solution.py:451
  18.9 13.4 %reduce_scatter.1 = (f32[2,64,512]{2,1,0:T(8,128)S(1)}, f32[2,16,128]{2,1,0:T(8,128)S(1)}) custom-call(f32[4,2,512,128]{3,2,1,0:T(8,128)S(1)} %get-tuple-element.32.spec_ref, f32[2,128,128]{2,1,0:T(8,128)S(1)} %get-tuple-element.33.pupil_ref), custom_call_target="tpu_custom_call" | custom-call | tf_op jit(solution)/shard_map/reduce_scatter/pallas_call | solution.py:585
  32.3 0.7 %store.1 = (f32[2,64,512]{2,1,0:T(8,128)}, f32[2,16,128]{2,1,0:T(8,128)}) custom-call(f32[2,64,512]{2,1,0:T(8,128)S(1)} %get-tuple-element.34.spec_ref, f32[2,16,128]{2,1,0:T(8,128)S(1)} %get-tuple-element.35.pupil_ref), custom_call_target="tpu_custom_call" | custom-call | tf_op jit(solution)/shard_map/store/pallas_call | solution.py:618

commit v8 on v7

--- a/solution.py
+++ b/solution.py
@@ -505,21 +505,19 @@
 
     used = [0]
 
-    def send(number, rows, other, code, scale, held_code, held_scale):
-        pair = []
-        here = pl.ds(8 * number, 8)
-        targets = held_code.at[rows], held_scale.at[here]
-        for src, dst in zip((scale.at[here], code.at[rows]), reversed(targets)):
-            sem = used[0]
-            used[0] += 1
-            pair.append(
-                pltpu.make_async_remote_copy(
-                    src_ref=src, dst_ref=dst, send_sem=send_sems.at[sem], recv_sem=recv_sems.at[sem],
-                    device_id={"led": other}, device_id_type=MESH,
-                )
-            )
-            pair[-1].start()
-        return pair, targets
+    def remote(src, dst, other):
+        sem = used[0]
+        used[0] += 1
+        copy = pltpu.make_async_remote_copy(
+            src_ref=src, dst_ref=dst, send_sem=send_sems.at[sem], recv_sem=recv_sems.at[sem],
+            device_id={"led": other}, device_id_type=MESH,
+        )
+        copy.start()
+        return copy
+
+    def first_scale(number):
+        slot = number if number >= SENT_A else number % (XS - 1) * 2 + number // (XS - 1)
+        return pl.ds(8 * slot, 8)
 
     def arrive(message, sent=False):
         for copy in message[0]:
@@ -529,16 +527,24 @@
         return message[1]
 
     def first(number, other):
-        return send(number, first_rows(number), other, codes, scales, held, held_scales)
+        here = first_rows(number)
+        return [remote(codes.at[here], held.at[here], other)], (held.at[here], held_scales.at[first_scale(number)])
+
+    def first_scales(start, rows, other):
+        here = pl.ds(start, rows)
+        return remote(scales.at[here], held_scales.at[here], other)
 
     def second(number, other):
-        return send(number, second_rows(number), other, codes2, scales2, held2, held_scales2)
+        here, scale = second_rows(number), pl.ds(8 * number, 8)
+        targets = held2.at[here], held_scales2.at[scale]
+        copies = [remote(scales2.at[scale], targets[1], other), remote(codes2.at[here], targets[0], other)]
+        return copies, targets
 
     hops = (1, 0, 2)
     mine = dest_of(line, place)
 
     def encode_first(number, bundle, dest):
-        encode(bundle, dest, [], codes.at[first_rows(number)], scales.at[pl.ds(8 * number, 8)])
+        encode(bundle, dest, [], codes.at[first_rows(number)], scales.at[first_scale(number)])
 
     for hop in hops:
         encode_first(SENT_A + hop, BUNDLE_B, dest_of(line + 1, place + 1 + hop))
@@ -549,6 +555,8 @@
     pl.semaphore_wait(barrier, XS)
 
     first_b, first_a, last_a, second_b = {}, {}, {}, {}
+    scales_b = first_scales(8 * SENT_A, 8 * SENT_B, opposite)
+    scales_a = [first_scales(16 * hop, 16, beside[hop]) for hop in hops]
     for hop in hops:
         first_b[hop] = first(SENT_A + hop, opposite)
         first_a[hop] = first(hop, beside[hop])
@@ -564,7 +572,10 @@
         encode(BUNDLE_B, beside[hop], parts, codes2.at[second_rows(1 + hop)], scales2.at[pl.ds(8 * (1 + hop), 8)])
         second_b[hop] = second(1 + hop, beside[hop])
 
+    scales_b.wait()
     pass_on(hops[0])
+    for copy in scales_a:
+        copy.wait()
     parts = [arrive(first_a[hop], sent=True) for hop in hops]
     encode(BUNDLE_A, opposite, parts, codes2.at[second_rows(0)], scales2.at[pl.ds(0, 8)])
     second_a = second(0, opposite)

time: 33.4 us -> 34.3 us (1.027); the launches traced: 33 us -> 34.7 us
  Pallas kernels: 32.3 us -> 34 us
    pallas_call x1, Pallas kernels: 4.33 us -> 6.37 us  [backward_call(): pl.pallas_call(partial(backward_kernel, scale), out_shape=(pltpu.VMEM(pla...]
    pallas_call x1, Pallas kernels: 13.4 us -> 13 us  [gather_call(): pl.pallas_call(gather_kernel, out_shape=(pltpu.VMEM((2, SPEC_ROWS, BLOCKS...]
where the time goes in v8:
time: 34.3 us; the launch traced here: 34.7 us
  Pallas kernels  34 us (99%)
  between operations  0.65 us (2%)
    pallas_call x1, Pallas kernels, forward_call(): pl.pallas_call(partial(forward_kernel, scale), out_shape=(pltpu.VMEM((2,...  13.9 us
    pallas_call x1, Pallas kernels, gather_call(): pl.pallas_call(gather_kernel, out_shape=(pltpu.VMEM((2, SPEC_ROWS, BLOCKS...  13 us
    pallas_call x1, Pallas kernels, backward_call(): pl.pallas_call(partial(backward_kernel, scale), out_shape=(pltpu.VMEM(pla...  6.37 us
    pallas_call x1, Pallas kernels, store_call(): pl.pallas_call(store_kernel, out_shape=(jax.ShapeDtypeStruct(spec_share.s...  0.72 us

profile of v8, /device:TPU:1, one launch (start us, length us, event | category | flops | bytes accessed | tf_op | source)
XLA Modules:
  0.0 34.7 jit_solution(15726340922590495147)
XLA Ops:
  0.6 13.9 %forward.1 = (bf16[2,29,2,96,128]{4,3,2,1,0:T(8,128)(2,1)S(1)}, f32[29,2,32,128]{3,2,1,0:T(8,128)S(1)}, bf16[2,28,16,128]{3,2,1,0:T(8,128)(2,1)S(1)}, bf16[28,16...) custom-call(s32[2,28]{1,0:T(2,128)} %bitcast.9, ...), custom_call_target="tpu_custom_call" | custom-call | tf_op jit(solution)/shard_map/forward/pallas_call | solution.py:414
  14.6 6.4 %backward.1 = (f32[4,2,512,128]{3,2,1,0:T(8,128)S(1)}, f32[2,128,128]{2,1,0:T(8,128)S(1)}) custom-call(s32[2,28]{1,0:T(2,128)S(4)} %get-tuple-element.20.offsets_ref, s32[63]{0:T(128)S(4)} %get-tuple-element.21.widths_ref, s32[28]{0:T(128)S(4)} %get-tuple-element.22.live_ref, f32[4,2,512,128]{3,2,1,0:T(8,128)S(1)} %get-tuple-element.23.planes, ...), custom_call_target="tpu_custom_call" | custom-call | tf_op jit(solution)/shard_map/backward/pallas_call | solution.py:451
  20.9 13.0 %reduce_scatter.1 = (f32[2,64,512]{2,1,0:T(8,128)S(1)}, f32[2,16,128]{2,1,0:T(8,128)S(1)}) custom-call(f32[4,2,512,128]{3,2,1,0:T(8,128)S(1)} %get-tuple-element.32.spec_ref, f32[2,128,128]{2,1,0:T(8,128)S(1)} %get-tuple-element.33.pupil_ref), custom_call_target="tpu_custom_call" | custom-call | tf_op jit(solution)/shard_map/reduce_scatter/pallas_call | solution.py:596
  33.9 0.7 %store.1 = (f32[2,64,512]{2,1,0:T(8,128)}, f32[2,16,128]{2,1,0:T(8,128)}) custom-call(f32[2,64,512]{2,1,0:T(8,128)S(1)} %get-tuple-element.34.spec_ref, f32[2,16,128]{2,1,0:T(8,128)S(1)} %get-tuple-element.35.pupil_ref), custom_call_target="tpu_custom_call" | custom-call | tf_op jit(solution)/shard_map/store/pallas_call | solution.py:629
